TPU v7x, 256 devices: a whole 4x4x8 slice. The times are simulated.
256 devices in a mesh: band: 8 (over z), pw: 32 (over x, y, core).
Axes of the slice: x: 4, y: 4, z: 8, core: 2. Of those that a mesh axis runs over, the one named last changes fastest.
Arguments:
- coeffs: float32 [2, 16, 114688], P(None, 'band', 'pw'), may hold values from -6 to 6
- occupation: float32 [16], P('band'), may hold values from 0.5 to 2
- stick_columns: int32 [3072], replicated, may hold values from 0 to 16383, as said below
- sphere_slots: int32 [114688], P('pw'), may hold values from 0 to 12287, as said below
- atom_sites: int32 [3, 1000], replicated, may hold values from 0 to 127
Outputs:
- new_coeffs: float32 [2, 16, 114688], P(None, 'band', 'pw')
- density: float32 [128, 128, 128], P('pw')
Inputs may be any that keep to these rules, and one draw needn't show every extreme that they name: `stick_columns`: all entries are distinct; each column's wrapped frequencies satisfy w(x)^2 + w(y)^2 <= 32^2. `sphere_slots`: within one block of 3584 entries the values are distinct; each names a point with w(x)^2 + w(y)^2 + w(z)^2 <= 32^2.
All inputs are finite; a program needn't handle non-finite values.
Results may differ from a plain program's by a relative error of at most 0.0003.
Values sent between devices are 32-bit elements; how exact they have to be, the bound alone decides.
A program may use at most 64 MiB of HBM per device.

v0:
```python
import math

import jax
import jax.numpy as jnp
from jax import lax
from jax.sharding import PartitionSpec as P

NG = 128


TIME_STEP = 0.2
EPSILON = 1e-06
HIGHEST = lax.Precision.HIGHEST


def wrapped(index):
    return jnp.where(index < NG // 2, index, index - NG)


def kinetic_factor():
    return 123.4 / (NG * NG)


def hartree_factor():
    return 0.1 * NG * NG


def form_factor(ksquare):
    spread_width = NG / 20.0
    return (
        -2.0
        * jnp.exp(-ksquare / (2.0 * spread_width * spread_width))
        / ((2.0 * math.pi) ** 1.5 * spread_width**3)
    )


def phase_table(kvalues, positions):
    angle = 2.0 * math.pi / NG * (kvalues[:, None] * positions[None, :] % NG).astype(jnp.float32)
    return (jnp.cos(angle), -jnp.sin(angle))


def fourier_table(direction):
    counter = jnp.arange(NG, dtype=jnp.int32)
    angle = 2.0 * math.pi / NG * (counter[:, None] * counter[None, :] % NG).astype(jnp.float32)
    return (jnp.cos(angle), direction * jnp.sin(angle))


def product(pattern, first, second):
    return jnp.einsum(pattern, first, second, precision=HIGHEST)


def complex_product(pattern, first, second):
    real_value = product(pattern, first[0], second[0]) - product(pattern, first[1], second[1])
    imag_value = product(pattern, first[0], second[1]) + product(pattern, first[1], second[0])
    return (real_value, imag_value)


def one_hot(values, width):
    return (values[:, None] == jnp.arange(width, dtype=jnp.int32)[None, :]).astype(jnp.float32)


def exponential_weights(first_energy, second_energy, spread):
    middle = 0.5 * (first_energy + second_energy)
    half_gap = 0.5 * (first_energy - second_energy)
    radius = jnp.sqrt(half_gap * half_gap + spread * spread)
    cosine = jnp.cos(TIME_STEP * radius)
    sine = jnp.sin(TIME_STEP * radius)
    along_first = sine * half_gap / radius
    along_second = sine * spread / radius
    phase_cos = jnp.cos(TIME_STEP * middle)
    phase_sin = jnp.sin(TIME_STEP * middle)
    weight_first = (
        phase_cos * cosine - phase_sin * along_first,
        -phase_cos * along_first - phase_sin * cosine,
    )
    weight_second = (-phase_sin * along_second, -phase_cos * along_second)
    return (weight_first, weight_second)


def local(coeffs, occupation, stick_columns, sphere_slots, atom_sites):
    parts = lax.axis_size("pw")
    bands = lax.axis_size("band")
    slab = NG // parts
    sticks_dev = stick_columns.shape[0] // parts
    total_pw = coeffs.shape[2] * parts
    orbitals_all = coeffs.shape[1] * bands
    place = lax.axis_index("pw")
    own_columns = lax.dynamic_slice_in_dim(stick_columns, place * sticks_dev, sticks_dev)
    slot_stick = sphere_slots // NG
    zvalue = sphere_slots % NG
    stick_hot = one_hot(slot_stick, sticks_dev)
    depth_hot = one_hot(zvalue, NG)
    column = jnp.sum(
        jnp.where(
            slot_stick[:, None] == jnp.arange(sticks_dev, dtype=jnp.int32)[None, :],
            own_columns[None, :],
            0,
        ),
        axis=1,
    )
    kinetic = kinetic_factor() * (
        wrapped(column // NG) ** 2 + wrapped(column % NG) ** 2 + wrapped(zvalue) ** 2
    ).astype(jnp.float32)
    row_hot = one_hot(stick_columns // NG, NG)
    col_hot = one_hot(stick_columns % NG, NG)
    inverse = fourier_table(1.0)
    forward = fourier_table(-1.0)
    to_grid = 1.0 / math.sqrt(total_pw)
    to_sphere = math.sqrt(total_pw) / NG**3

    def sticks_of(real_part, imag_part):
        stacked = jnp.stack([real_part, imag_part], axis=1)
        grid = product("js,bcjk->bcsk", stick_hot, stacked[:, :, :, None] * depth_hot[None, None])
        along_re, along_im = complex_product("bsk,kz->bzs", (grid[:, 0], grid[:, 1]), inverse)
        return jnp.stack([along_re, along_im], axis=1)

    def field_of(planes):
        plane_both = product("czsy,sx->czxy", planes[:, :, :, None] * col_hot[None, None], row_hot)
        rows = complex_product("zpq,qy->zpy", (plane_both[0], plane_both[1]), inverse)
        field_re, field_im = complex_product("zpy,px->zxy", rows, inverse)
        return (field_re * to_grid, field_im * to_grid)

    def back_to_sphere(partial_value):
        sticks = lax.all_to_all(partial_value, "pw", split_axis=3, concat_axis=2, tiled=True)
        along_re, along_im = complex_product("bzs,zk->bsk", (sticks[:, 0], sticks[:, 1]), forward)
        along_both = jnp.stack([along_re, along_im], axis=1)
        spread_out = product("js,bcsk->bcjk", stick_hot, along_both)
        picked = jnp.sum(spread_out * depth_hot[None, None], axis=3) * to_sphere
        return (picked[:, 0], picked[:, 1])

    coef_re = coeffs[0]
    coef_im = coeffs[1]
    planes_all = lax.all_to_all(
        sticks_of(coef_re, coef_im), "pw", split_axis=2, concat_axis=3, tiled=True
    )

    def add_density(total, item):
        planes, weight = item
        field_re, field_im = field_of(planes)
        return (total + weight * (field_re * field_re + field_im * field_im), None)

    partial_density = lax.scan(
        add_density, jnp.zeros((slab, NG, NG), jnp.float32), (planes_all, occupation)
    )[0]
    counter = jnp.arange(NG, dtype=jnp.int32)
    kx_global = place * slab + jnp.arange(slab, dtype=jnp.int32)
    phase_first = phase_table(kx_global, atom_sites[0])
    phase_second = phase_table(counter, atom_sites[1])
    phase_third = phase_table(counter, atom_sites[2])
    cross_re = (
        phase_third[0][:, None, :] * phase_first[0][None, :, :]
        - phase_third[1][:, None, :] * phase_first[1][None, :, :]
    )
    cross_im = (
        phase_third[0][:, None, :] * phase_first[1][None, :, :]
        + phase_third[1][:, None, :] * phase_first[0][None, :, :]
    )
    factor_re, factor_im = complex_product("pia,qa->piq", (cross_re, cross_im), phase_second)
    density_total = lax.psum(partial_density, "band")
    density = density_total / orbitals_all
    spec_re = product("zxy,yq->zxq", density, forward[0])
    spec_im = product("zxy,yq->zxq", density, forward[1])
    mixed = complex_product("zxq,xp->zpq", (spec_re, spec_im), forward)
    block = lax.all_to_all(jnp.stack(mixed), "pw", split_axis=2, concat_axis=1, tiled=True)
    spectrum = jnp.stack(complex_product("zib,zk->kib", (block[0], block[1]), forward))
    kz_wrap = wrapped(counter)[:, None, None]
    kx_wrap = wrapped(kx_global)[None, :, None]
    ky_wrap = wrapped(counter)[None, None, :]
    ksq_int = kz_wrap**2 + kx_wrap**2 + ky_wrap**2
    ksq_float = ksq_int.astype(jnp.float32)
    hartree = jnp.where(ksq_int > 0, hartree_factor() / jnp.maximum(ksq_float, 1.0), 0.0) / NG**3
    local_form = form_factor(ksq_float)
    total_re = hartree * spectrum[0] + local_form * factor_re
    total_im = hartree * spectrum[1] + local_form * factor_im
    back_depth = complex_product("kiq,kz->ziq", (total_re, total_im), inverse)
    block = lax.all_to_all(jnp.stack(back_depth), "pw", split_axis=1, concat_axis=2, tiled=True)
    rows_back = jnp.stack(complex_product("zpb,px->zxb", (block[0], block[1]), inverse))
    potential = product("zxq,qy->zxy", rows_back[0], inverse[0]) - product(
        "zxq,qy->zxy", rows_back[1], inverse[1]
    )

    def local_apply(planes):
        field_re, field_im = field_of(planes)
        turned = complex_product(
            "zxy,yq->zxq", (potential * field_re, potential * field_im), forward
        )
        out_re, out_im = complex_product("zxq,xp->zpq", turned, forward)
        gathered = product("czpq,sp->czsq", jnp.stack([out_re, out_im]), row_hot)
        return jnp.sum(gathered * col_hot[None, None], axis=3)

    def potential_part(planes_block):
        return back_to_sphere(lax.map(local_apply, planes_block))

    part_re, part_im = potential_part(planes_all)
    hit_re = kinetic * coef_re + part_re
    hit_im = kinetic * coef_im + part_im
    norm_raw, cross_raw = lax.psum(
        (
            jnp.sum(coef_re * coef_re + coef_im * coef_im, axis=1),
            jnp.sum(coef_re * hit_re + coef_im * hit_im, axis=1),
        ),
        "pw",
    )
    norm_sq = norm_raw + EPSILON
    norm = jnp.sqrt(norm_sq)
    first_energy = cross_raw / norm_sq
    rest_re = (hit_re - first_energy[:, None] * coef_re) / norm[:, None]
    rest_im = (hit_im - first_energy[:, None] * coef_im) / norm[:, None]
    rest_sq = lax.psum(jnp.sum(rest_re * rest_re + rest_im * rest_im, axis=1), "pw")
    spread = jnp.sqrt(rest_sq + EPSILON)
    next_re = rest_re / spread[:, None]
    next_im = rest_im / spread[:, None]
    back_re, back_im = potential_part(
        lax.all_to_all(sticks_of(next_re, next_im), "pw", split_axis=2, concat_axis=3, tiled=True)
    )
    applied = jnp.stack([back_re, back_im], axis=1)
    again_re = kinetic * next_re + applied[:, 0]
    again_im = kinetic * next_im + applied[:, 1]
    second_energy = lax.psum(jnp.sum(next_re * again_re + next_im * again_im, axis=1), "pw")
    weight_first, weight_second = exponential_weights(first_energy, second_energy, spread)
    first_re = weight_first[0][:, None]
    first_im = weight_first[1][:, None]
    second_re = (norm * weight_second[0])[:, None]
    second_im = (norm * weight_second[1])[:, None]
    new_re = first_re * coef_re - first_im * coef_im + (second_re * next_re - second_im * next_im)
    new_im = first_re * coef_im + first_im * coef_re + (second_re * next_im + second_im * next_re)
    return (jnp.stack([new_re, new_im]), density)


def solution(mesh):
    in_specs = (P(None, "band", "pw"), P("band"), P(), P("pw"), P())
    out_specs = (P(None, "band", "pw"), P("pw", None, None))
    return jax.shard_map(local, mesh=mesh, in_specs=in_specs, out_specs=out_specs, check_vma=False)
```

profile of v0, /device:TPU:1, one launch (start us, length us, event | category | flops | bytes accessed | tf_op | source)
XLA Modules:
  0.0 673.8 jit_solution(12256384620684377501)
XLA Ops:
  34.4 46.1 %while.40 = (s32[]{:T(128)}, f32[4,128,128]{1,2,0:T(8,128)S(1)}, f32[2]{0:T(128)S(1)}, f32[2,2,4,3072]{3,2,1,0:T(4,128)S(1)}, s32[3072]{0:T(1024)S(1)}, /*index=5*/s32[3072]{0:T(1024)S(1)}, s32[]{:T(128)}, s32[]{:T(128)}) while((s32[]{:T(128)}, f32[4,128,128]{1,2,0:T(8,128)S(1)}, f32[2]{0:T(128)S(1)}, ...), condition=%wide.region_2.3_spmd.clone.clone, body=%wide.region_1.2_spmd.clone.clone.sunk | while | flops 5644484608 | bytes 9756787 | solution.py:142
  45.5 10.0 %fusion.1129 = f32[2,4,128,128]{2,3,1,0:T(8,128)S(1)} fusion(f32[3072,128]{0,1:T(8,128)S(1)} %fusion.1128, f32[2,4,3072]{2,1,0:T(4,128)S(1)} %dynamic-slice_bitcast_fusion.8, s32[3072]{0:T(1024)S(1)} %get-tuple-element.720), kind=kOutput, calls=%fused_computation.325.clone.1 | convolution fusion | flops 4835770368 | bytes 2207744 | tf_op jit(solution)/shard_map/while/body/eval_jaxpr/czsy,sx->czxy/dot_general | solution.py:49
  62.9 10.0 %fusion.1129 = f32[2,4,128,128]{2,3,1,0:T(8,128)S(1)} fusion(f32[3072,128]{0,1:T(8,128)S(1)} %fusion.1128, f32[2,4,3072]{2,1,0:T(4,128)S(1)} %dynamic-slice_bitcast_fusion.8, s32[3072]{0:T(1024)S(1)} %get-tuple-element.720), kind=kOutput, calls=%fused_computation.325.clone.1 | convolution fusion | flops 4835770368 | bytes 2207744 | tf_op jit(solution)/shard_map/while/body/eval_jaxpr/czsy,sx->czxy/dot_general | solution.py:49
  88.9 63.1 %all-reduce.3.cloned.1.call-done = f32[4,128,128]{2,1,0:T(8,128)} async-done(((f32[4,128,128]{2,1,0:T(8,128)}), f32[4,128,128]{2,1,0:T(8,128)}) %all-reduce.3.cloned.1.call-update) | async-done | bytes 262160 | tf_op jit(solution)/shard_map/psum | solution.py:159
  158.1 12.2 %all-to-all-start.1 = ((f32[2,4,128,128]{3,1,0,2:T(4,128)}), f32[2,4,128,128]{3,1,0,2:T(4,128)S(1)}, u32[]{:S(2)}, u32[]{:S(2)}) async-start(f32[2,4,128,128]{3,1,0,2:T(4,128)} %copy.275), calls=%async_computation.1 | async-start | bytes 1048576 | tf_op jit(solution)/shard_map/all_to_all | solution.py:164
  198.5 11.2 %all-to-all-done.2 = f32[2,128,4,128]{3,2,0,1:T(4,128)S(1)} async-done(((f32[2,128,4,128]{3,2,0,1:T(4,128)}), f32[2,128,4,128]{3,2,0,1:T(4,128)S(1)}, u32[]{:S(2)}, u32[]{:S(2)}) %all-to-all-start.2) | async-done | bytes 524320 | tf_op jit(solution)/shard_map/all_to_all | solution.py:176
  213.9 67.7 %while.38 = (s32[]{:T(128)}, f32[2,2,4,3072]{3,2,1,0:T(4,128)S(1)}, f32[2,2,4,3072]{3,2,1,0:T(4,128)S(1)}, f32[4,128,128]{1,2,0:T(8,128)S(1)}, s32[3072]{0:T(1024)S(1)}, /*index=5*/s32[3072]{0:T(1024)S(1)}, s32[]{:T(128)}) while((s32[]{:T(128)}, f32[2,2,4,3072]{3,2,1,0:T(4,128)S(1)}, f32[2,2,4,3072]{3,2,1,0:T(4,128)S(1)}, ...), condition=%wide.region_6.7_spmd.clone.clone, body=%wide.region_4.6_spmd.clone.clone.sunk | while | flops 11290714112 | bytes 17403988 | solution.py:192
  214.3 10.0 %fusion.1053 = f32[2,4,128,128]{2,3,1,0:T(8,128)S(1)} fusion(f32[3072,128]{0,1:T(8,128)S(1)} %fusion.1052, f32[2,4,3072]{2,1,0:T(4,128)S(1)} %dynamic-slice_bitcast_fusion.6, s32[3072]{0:T(1024)S(1)} %get-tuple-element.742), kind=kOutput, calls=%fused_computation.27.clone.1 | convolution fusion | flops 4835770368 | bytes 2207744 | tf_op jit(solution)/shard_map/while/body/eval_jaxpr/czsy,sx->czxy/dot_general | solution.py:49
  236.0 11.6 %fusion.1066 = f32[2,4,3072]{2,1,0:T(4,128)S(1)} fusion(f32[3072,128]{0,1:T(8,128)S(1)} %fusion.1052, s32[3072]{0:T(1024)S(1)} %get-tuple-element.742, f32[1,4,128,128]{2,3,1,0:T(8,128)S(1)} %fusion.1063, f32[1,4,128,128]{2,3,1,0:T(8,128)S(1)} %fusion.1065), kind=kOutput, calls=%fused_computation.15.clone.1 | convolution fusion | flops 4839022592 | bytes 2207744 | tf_op jit(solution)/shard_map/while/body/eval_jaxpr/czpq,sp->czsq/dot_general | solution.py:49
  247.9 10.0 %fusion.1053 = f32[2,4,128,128]{2,3,1,0:T(8,128)S(1)} fusion(f32[3072,128]{0,1:T(8,128)S(1)} %fusion.1052, f32[2,4,3072]{2,1,0:T(4,128)S(1)} %dynamic-slice_bitcast_fusion.6, s32[3072]{0:T(1024)S(1)} %get-tuple-element.742), kind=kOutput, calls=%fused_computation.27.clone.1 | convolution fusion | flops 4835770368 | bytes 2207744 | tf_op jit(solution)/shard_map/while/body/eval_jaxpr/czsy,sx->czxy/dot_general | solution.py:49
  269.6 11.6 %fusion.1066 = f32[2,4,3072]{2,1,0:T(4,128)S(1)} fusion(f32[3072,128]{0,1:T(8,128)S(1)} %fusion.1052, s32[3072]{0:T(1024)S(1)} %get-tuple-element.742, f32[1,4,128,128]{2,3,1,0:T(8,128)S(1)} %fusion.1063, f32[1,4,128,128]{2,3,1,0:T(8,128)S(1)} %fusion.1065), kind=kOutput, calls=%fused_computation.15.clone.1 | convolution fusion | flops 4839022592 | bytes 2207744 | tf_op jit(solution)/shard_map/while/body/eval_jaxpr/czpq,sp->czsq/dot_general | solution.py:49
  287.8 9.9 %reshape.501 = f32[32,1,1536]{2,1,0:T(1,128)} reshape(f32[3072,2,2,4]{3,2,1,0:T(2,128)} %bitcast.794) | data formatting | bytes 393216
  311.5 11.4 %reshape.502 = f32[3072,2,2,4]{3,2,1,0:T(2,128)} reshape(f32[32,1536]{1,0:T(8,128)S(1)} %reduce) | data formatting | bytes 393216
  335.9 62.3 %all-reduce = (f32[2]{0:T(128)S(1)}, f32[2]{0:T(128)S(1)}) all-reduce(f32[2]{0:T(128)S(1)} %get-tuple-element.510, f32[2]{0:T(128)S(1)} %get-tuple-element.509), channel_id=1, replica_groups=mesh['band'=8,'pw'=32] {'pw'}, use_global_device_ids=true, to_apply=%region_9.10 | all-reduce | flops 4 | bytes 32 | tf_op jit(solution)/shard_map/psum | solution.py:197
  398.5 64.7 %psum.38 = f32[2]{0:T(128)S(1)} all-reduce(f32[2]{0:T(128)S(1)} %get-tuple-element.557), channel_id=1, replica_groups=mesh['band'=8,'pw'=32] {'pw'}, use_global_device_ids=true, to_apply=%region_13.14 | all-reduce | flops 2 | bytes 16 | tf_op jit(solution)/shard_map/psum | solution.py:209
  469.9 12.4 %all_to_all.102 = f32[2,2,128,96]{3,0,1,2:T(2,128)S(1)} all-to-all(f32[2,2,128,96]{3,0,1,2:T(2,128)S(1)} %copy.299), channel_id=1, replica_groups=mesh['band'=8,'pw'=32] {'pw'}, dimensions={2} | all-to-all | bytes 393216 | tf_op jit(solution)/shard_map/all_to_all | solution.py:214
  482.6 67.7 %while.39 = (s32[]{:T(128)}, f32[2,2,4,3072]{3,2,1,0:T(4,128)S(1)}, f32[2,2,4,3072]{3,2,1,0:T(4,128)S(1)}, f32[4,128,128]{1,2,0:T(8,128)S(1)}, s32[3072]{0:T(1024)S(1)}, /*index=5*/s32[3072]{0:T(1024)S(1)}, s32[]{:T(128)}) while((s32[]{:T(128)}, f32[2,2,4,3072]{3,2,1,0:T(4,128)S(1)}, ...), condition=%wide.region_16.17_spmd.clone.clone, body=%wide.region_14.16_spmd.clone.clone.sunk | while | flops 11290714112 | bytes 17403988 | solution.py:192
  483.0 10.0 %fusion.1100 = f32[2,4,128,128]{2,3,1,0:T(8,128)S(1)} fusion(f32[3072,128]{0,1:T(8,128)S(1)} %fusion.1099, f32[2,4,3072]{2,1,0:T(4,128)S(1)} %dynamic-slice_bitcast_fusion.7, s32[3072]{0:T(1024)S(1)} %get-tuple-element.763), kind=kOutput, calls=%fused_computation.178.clone.1 | convolution fusion | flops 4835770368 | bytes 2207744 | tf_op jit(solution)/shard_map/while/body/eval_jaxpr/czsy,sx->czxy/dot_general | solution.py:49
  504.7 11.6 %fusion.1113 = f32[2,4,3072]{2,1,0:T(4,128)S(1)} fusion(f32[3072,128]{0,1:T(8,128)S(1)} %fusion.1099, s32[3072]{0:T(1024)S(1)} %get-tuple-element.763, f32[1,4,128,128]{2,3,1,0:T(8,128)S(1)} %fusion.1110, f32[1,4,128,128]{2,3,1,0:T(8,128)S(1)} %fusion.1112), kind=kOutput, calls=%fused_computation.166.clone.1 | convolution fusion | flops 4839022592 | bytes 2207744 | tf_op jit(solution)/shard_map/while/body/eval_jaxpr/czpq,sp->czsq/dot_general | solution.py:49
  516.6 10.0 %fusion.1100 = f32[2,4,128,128]{2,3,1,0:T(8,128)S(1)} fusion(f32[3072,128]{0,1:T(8,128)S(1)} %fusion.1099, f32[2,4,3072]{2,1,0:T(4,128)S(1)} %dynamic-slice_bitcast_fusion.7, s32[3072]{0:T(1024)S(1)} %get-tuple-element.763), kind=kOutput, calls=%fused_computation.178.clone.1 | convolution fusion | flops 4835770368 | bytes 2207744 | tf_op jit(solution)/shard_map/while/body/eval_jaxpr/czsy,sx->czxy/dot_general | solution.py:49
  538.3 11.6 %fusion.1113 = f32[2,4,3072]{2,1,0:T(4,128)S(1)} fusion(f32[3072,128]{0,1:T(8,128)S(1)} %fusion.1099, s32[3072]{0:T(1024)S(1)} %get-tuple-element.763, f32[1,4,128,128]{2,3,1,0:T(8,128)S(1)} %fusion.1110, f32[1,4,128,128]{2,3,1,0:T(8,128)S(1)} %fusion.1112), kind=kOutput, calls=%fused_computation.166.clone.1 | convolution fusion | flops 4839022592 | bytes 2207744 | tf_op jit(solution)/shard_map/while/body/eval_jaxpr/czpq,sp->czsq/dot_general | solution.py:49
  565.7 12.0 %all_to_all.103 = f32[32,1,1536]{2,1,0:T(1,128)S(1)} all-to-all(f32[32,1,1536]{2,1,0:T(1,128)S(1)} %reshape.503), channel_id=1, replica_groups=mesh['band'=8,'pw'=32] {'pw'}, dimensions={0} | all-to-all | bytes 393216 | tf_op jit(solution)/shard_map/all_to_all | solution.py:124
  578.8 11.4 %reshape.504 = f32[3072,2,2,4]{3,2,1,0:T(2,128)} reshape(f32[32,1536]{1,0:T(8,128)S(1)} %reduce.1) | data formatting | bytes 393216
  603.3 62.3 %psum.39 = f32[2]{0:T(128)S(1)} all-reduce(f32[2]{0:T(128)S(1)} %fusion.653), channel_id=1, replica_groups=mesh['band'=8,'pw'=32] {'pw'}, use_global_device_ids=true, to_apply=%region_19.20 | all-reduce | flops 2 | bytes 16 | tf_op jit(solution)/shard_map/psum | solution.py:219
  (240 shorter events, 206.2 us)
Async XLA Ops:
  13.2 11.9 %copy-start.7 = (s32[3072]{0:T(1024)S(1)}, s32[3072]{0:T(1024)}, u32[]{:S(2)}) copy-start(s32[3072]{0:T(1024)} %param.13) | copy-start | bytes 36868
  13.2 12.0 %copy-start.8 = (s32[3,1000]{1,0:T(4,128)S(1)}, s32[3,1000]{1,0:T(4,128)}, u32[]{:S(2)}) copy-start(s32[3,1000]{1,0:T(4,128)} %param.15) | copy-start | bytes 36004
  16.1 18.0 %all-to-all-start = ((f32[2,2,128,96]{3,0,1,2:T(2,128)}), f32[2,2,128,96]{3,0,1,2:T(2,128)S(1)}, u32[]{:S(2)}, u32[]{:S(2)}) async-start(f32[2,2,128,96]{3,0,1,2:T(2,128)} %copy.267), calls=%async_computation | async-start | bytes 524288 | tf_op jit(solution)/shard_map/all_to_all | solution.py:133
  24.7 127.3 %all-reduce.3.cloned.1.call-start = ((), (), s32[]{:S(2)}) async-start(), calls=%async_computation.6 | async-start | bytes 524288 | tf_op jit(solution)/shard_map/psum | solution.py:159
  27.3 6.7 copy-start.2
  27.3 6.7 copy-start.4
  27.6 6.8 %copy-start.9 = (f32[2]{0:T(128)S(1)}, f32[2]{0:T(128)}, u32[]{:S(2)}) copy-start(f32[2]{0:T(128)} %param.12) | copy-start | bytes 28
  34.4 47.0 %copy-start.12 = (f32[128,4,128]{2,0,1:T(8,128)S(1)}, f32[128,4,128]{2,0,1:T(8,128)}, u32[]{:S(2)}) copy-start(f32[128,4,128]{2,0,1:T(8,128)} %fusion.426) | copy-start | bytes 786436
  153.0 4.0 copy-start
  156.3 14.1 %copy-start.3 = (f32[128,1000]{0,1:T(8,128)S(1)}, f32[128,1000]{0,1:T(8,128)}, u32[]{:S(2)}) copy-start(f32[128,1000]{0,1:T(8,128)} %copy-done.2) | copy-start | bytes 1536004
  158.1 25.5 %all-to-all-start.1 = ((f32[2,4,128,128]{3,1,0,2:T(4,128)}), f32[2,4,128,128]{3,1,0,2:T(4,128)S(1)}, u32[]{:S(2)}, u32[]{:S(2)}) async-start(f32[2,4,128,128]{3,1,0,2:T(4,128)} %copy.275), calls=%async_computation.1 | async-start | bytes 1048576 | tf_op jit(solution)/shard_map/all_to_all | solution.py:164
  170.3 6.8 %copy-start.5 = (f32[128,1000]{0,1:T(8,128)S(1)}, f32[128,1000]{0,1:T(8,128)}, u32[]{:S(2)}) copy-start(f32[128,1000]{0,1:T(8,128)} %copy-done.4) | copy-start | bytes 1536004
  183.6 1.9 copy-start.11
  183.7 3.8 copy-start.10
  190.7 19.0 %all-to-all-start.2 = ((f32[2,128,4,128]{3,2,0,1:T(4,128)}), f32[2,128,4,128]{3,2,0,1:T(4,128)S(1)}, u32[]{:S(2)}, u32[]{:S(2)}) async-start(f32[2,128,4,128]{3,2,0,1:T(4,128)} %copy.285), calls=%async_computation.2 | async-start | bytes 1048576 | tf_op jit(solution)/shard_map/all_to_all | solution.py:176
  287.8 13.8 %copy-start.6 = (s32[3584]{0:T(1024)S(1)}, s32[3584]{0:T(1024)}, u32[]{:S(2)}) copy-start(s32[3584]{0:T(1024)} %param.14) | copy-start | bytes 43012
  297.6 12.1 %all-to-all-start.3 = ((f32[32,1,1536]{2,1,0:T(1,128)}), f32[32,1,1536]{2,1,0:T(1,128)S(1)}, u32[]{:S(2)}, u32[]{:S(2)}) async-start(f32[32,1,1536]{2,1,0:T(1,128)} %reshape.501), calls=%async_computation.3 | async-start | bytes 393216 | tf_op jit(solution)/shard_map/all_to_all | solution.py:124
  332.0 3.8 copy-start.1
Sparse Core Ops, SparseCore 0:
  81.5 70.5 all-reduce.2
where the time goes:
time: 680 us; the launch traced here: 674 us
  matrix products  230 us (34%)
  blocking collectives  214 us (31%)
  waiting for transfers between devices  82.5 us (12%)
  local copies, waits for them, and re-layouts  77 us (11%)
  starting transfers between devices  32.5 us (5%)
  between operations  15.1 us (2%)
  loops' own time  13.3 us (2%)
  other arithmetic  9.44 us (1%)
    dot_general x134, matrix products, product(): return jnp.einsum(pattern, first, second, precision=HIGHEST)  230 us
    psum x1, blocking collectives, local(): lax.psum(jnp.sum(rest_re * rest_re + rest_im * rest_im, axis=1), 'pw')  64.7 us
    psum x1, waiting for transfers between devices, local(): density_total = lax.psum(partial_density, 'band')  63.1 us
    psum x1, blocking collectives, local(): lax.psum(jnp.sum(next_re * again_re + next_im * again_im, axis=1), 'pw')  62.3 us
    psum x1, blocking collectives, local(): lax.psum((jnp.sum(coef_re * coef_re + coef_im * coef_im, axis=1), jnp.sum...  62.3 us
    unnamed x32, local copies, waits for them, and re-layouts  42.7 us
    all_to_all x3, local copies, waits for them, and re-layouts, back_to_sphere(): lax.all_to_all(partial_value, 'pw', split_axis=3, concat_axis=2, tiled=True)  14.7 us
  transfers between devices with their start and end apart: 5, of which 3 were waited for; matrix products, arithmetic and copies ran while one was open for 4% of the time, Pallas kernels for 0%

commit v1 on v0

v1 whole, which is shorter than its diff:
```python
import functools
import math

import jax
import jax.numpy as jnp
import numpy as np
import ml_dtypes
from jax import lax
from jax.experimental import pallas as pl
from jax.experimental.pallas import tpu as pltpu
from jax.sharding import PartitionSpec as P

MESH = pl.DeviceIdType.MESH
F32 = jnp.float32
BF16 = jnp.bfloat16

NG = 128
NP = 32
NB = 8
NPW_DEV = 3584
NPW = NPW_DEV * NP
ST = 96
KZ = 80
NR = 24
TIME_STEP = 0.2
EPSILON = 1e-06
STEP = 2.0 * math.pi / NG
WIDTH = NG / 20.0
FORM = -2.0 / ((2.0 * math.pi) ** 1.5 * WIDTH**3)
TO_GRID = 1.0 / math.sqrt(NPW)
TO_SPHERE = math.sqrt(NPW) / NG**3
HARTREE = 0.1 * NG * NG

A1, RS, A2, A3, AGV, AGD, A4, A5, AR = 0, 2, 3, 4, 5, 6, 7, 9, 11
N_SEM = 12


def parts(x):
    hi = x.astype(np.float32).astype(ml_dtypes.bfloat16)
    lo = (x - hi.astype(np.float64)).astype(np.float32).astype(ml_dtypes.bfloat16)
    return hi, lo


def left_table(x):
    hi, lo = parts(x)
    return np.concatenate([hi, hi, lo], axis=1)


def right_table(x):
    hi, lo = parts(x)
    return np.concatenate([hi, hi, lo], axis=0)


def phases(rows, cols):
    angle = STEP * np.mod(np.outer(rows, cols), NG)
    return np.cos(angle), np.sin(angle)


def build_tables():
    grid = np.arange(NG)
    kz_mask = (np.arange(KZ) <= 64).astype(np.float64)
    kz = np.arange(KZ) - 32
    tables = {}
    c, s = phases(grid, kz)
    c, s = c * kz_mask, s * kz_mask
    up = np.zeros((NG, 2, 2, KZ))
    up[:, 0, 0], up[:, 0, 1], up[:, 1, 0], up[:, 1, 1] = c, -s, s, c
    tables["z_up"] = left_table(up.reshape(2 * NG, 2 * KZ))
    down = np.zeros((2, KZ, NG, 2))
    down[0, :, :, 0], down[0, :, :, 1] = c.T, s.T
    down[1, :, :, 0], down[1, :, :, 1] = -s.T, c.T
    tables["z_down"] = left_table(down.reshape(2 * KZ, 2 * NG))

    wy = np.tile(np.arange(64) - 32, (4, 1))
    wy[1, 0] = 32
    y_up = np.zeros((4, 64, 2, 4, NG))
    y_down = np.zeros((4, NG, 2, 4, 64))
    for j in range(4):
        c, s = phases(wy[j], grid)
        y_up[j, :, 0, j], y_up[j, :, 1, j] = c, s
        y_down[j, :, 0, j], y_down[j, :, 1, j] = c.T, s.T
    tables["y_up"] = right_table(y_up.reshape(256, 1024))
    tables["y_down"] = right_table(y_down.reshape(512, 512))

    wx = np.zeros((4, NR))
    xm = np.zeros((4, NR))
    for j in range(4):
        for r in range(16):
            wx[j, r], xm[j, r] = 4 * r + j - 32, 1.0
    wx[0, 16], xm[0, 16] = 32, 1.0
    wx[1, 16], xm[1, 16] = 0, 1.0
    c, s = phases(grid, wx.reshape(-1))
    c, s = c * xm.reshape(-1), s * xm.reshape(-1)
    x_up = np.zeros((2, NG, 2, 4 * NR))
    x_up[0, :, 0], x_up[0, :, 1], x_up[1, :, 0], x_up[1, :, 1] = c, -s, s, c
    tables["x_up"] = left_table(TO_GRID * x_up.reshape(2 * NG, 8 * NR))
    x_down = np.zeros((2, 4 * NR, 2, NG))
    x_down[0, :, 0], x_down[0, :, 1], x_down[1, :, 0], x_down[1, :, 1] = c.T, s.T, -s.T, c.T
    tables["x_down"] = left_table(TO_SPHERE * x_down.reshape(8 * NR, 2 * NG))

    c, s = phases(grid, np.arange(64))
    fwd = np.zeros((NG, 2, 64))
    fwd[:, 0], fwd[:, 1] = c, -s
    sign = np.where(grid % 2 == 0, 1.0, -1.0)
    fwd[:, 1, 0] = sign
    tables["py"] = right_table(fwd.reshape(NG, NG))
    inv = np.zeros((2, 64, NG))
    inv[0], inv[1] = 2.0 * c.T, -2.0 * s.T
    inv[0, 0], inv[1, 0] = 1.0, sign
    tables["piy"] = right_table(inv.reshape(NG, NG))
    c, s = phases(grid, grid)
    tables["px"] = left_table(np.concatenate([c, s], axis=1))
    tables["pix"] = left_table(np.concatenate([c, -s], axis=1))
    pairs = np.concatenate([grid[0::2], grid[1::2]])
    tables["pixp"] = left_table(np.concatenate([c[:, pairs], -s[:, pairs]], axis=1))
    pair = np.eye(2)
    cc, ss = np.kron(c, pair), np.kron(s, pair)
    tables["pz"] = left_table(np.concatenate([cc, ss], axis=1))
    tables["piz"] = left_table(np.concatenate([cc, -ss], axis=1))

    wk = np.where(grid < 64, grid, grid - NG)
    gauss = np.exp(-(wk**2) / (2.0 * WIDTH * WIDTH))
    g = np.cos(STEP * np.mod(np.outer(grid, grid), NG)) @ gauss
    circ = g[np.mod(grid[:, None] - grid[None, :], NG)]
    tables["circ"] = np.concatenate(parts(circ), axis=1)
    return tables


TABLES = build_tables()
NAMES = ("z_up", "y_up", "x_up", "py", "px", "circ", "pz", "piz", "pixp", "piy", "x_down", "y_down", "z_down", "pix")


def mm(a, b):
    return lax.dot_general(a, b, (((1,), (0,)), ((), ())), preferred_element_type=F32)


def mm_nt(a, b):
    return lax.dot_general(a, b, (((1,), (1,)), ((), ())), preferred_element_type=F32)


def split(x):
    hi = x.astype(BF16)
    return hi, (x - hi.astype(F32)).astype(BF16)


def stack_rows(x):
    hi, lo = split(x)
    return jnp.concatenate([hi, lo, hi], axis=0)


def stack_lanes(x):
    hi, lo = split(x)
    return jnp.concatenate([hi, lo, hi], axis=1)


def total(x):
    return jnp.sum(jnp.sum(x, axis=0, keepdims=True), axis=1, keepdims=True)


def iota(shape, axis):
    return lax.broadcasted_iota(jnp.int32, shape, axis)


def wrapped(x):
    return jnp.where(x < NG // 2, x, x - NG)


def turned(x):
    sgn = jnp.where(iota((1, 128), 1) < 64, 1.0, -1.0).astype(F32)
    return pltpu.roll(x, 64, 1) * sgn


def lanes_to_rows(x):
    return jnp.concatenate([x[:, i * 128 : (i + 1) * 128] for i in range(4)], axis=0)


def rows_to_lanes(x):
    return jnp.concatenate([x[i * 128 : (i + 1) * 128] for i in range(4)], axis=1)


def exponential_weights(first_energy, second_energy, spread):
    middle = 0.5 * (first_energy + second_energy)
    half_gap = 0.5 * (first_energy - second_energy)
    radius = jnp.sqrt(half_gap * half_gap + spread * spread)
    cosine = jnp.cos(TIME_STEP * radius)
    sine = jnp.sin(TIME_STEP * radius)
    along_first = sine * half_gap / radius
    along_second = sine * spread / radius
    phase_cos = jnp.cos(TIME_STEP * middle)
    phase_sin = jnp.sin(TIME_STEP * middle)
    weight_first = (
        phase_cos * cosine - phase_sin * along_first,
        -phase_cos * along_first - phase_sin * cosine,
    )
    weight_second = (-phase_sin * along_second, -phase_cos * along_second)
    return (weight_first, weight_second)


def kernel(coeffs_in, occ_in, cols_in, slots_in, atoms_in, *refs):
    t = dict(zip(NAMES, refs[: len(NAMES)]))
    held = dict(zip(NAMES, refs[-len(NAMES) - 1 : -1]))
    tsem = refs[-1]
    (new_out, dens_out, coeffs, occ, cols, slots, atoms, new, dens_val, sh, cz, kin, tt, mt, field, slv, cpad, apad, vloc, pot, wvec, sb1, rb1, xb, rsb, sbuf, tb, rb2,
     ub, rbv, dk, sb4, rb4, sb5, rb5, sbr, rbr, gz, ssem, rsem, isem, osem) = refs[len(NAMES) : -len(NAMES) - 1]
    me = lax.axis_index("pw")
    band = lax.axis_index("band")

    loads = {k: pltpu.make_async_copy(t[k], held[k], tsem.at[i]) for i, k in enumerate(NAMES)}
    inputs = (slots_in, slots), (coeffs_in, coeffs), (cols_in, cols), (occ_in, occ), (atoms_in, atoms)
    inputs = [pltpu.make_async_copy(a, b, isem.at[i]) for i, (a, b) in enumerate(inputs)]
    for copy in inputs:
        copy.start()

    def table(k):
        if k in loads:
            loads.pop(k).wait()
        return held[k][...]

    barrier = pltpu.get_barrier_semaphore()

    def greet_pw(i, carry):
        pl.semaphore_signal(barrier, inc=1, device_id={"pw": lax.rem(me + i, NP)}, device_id_type=MESH)
        return carry

    def greet_band(i, carry):
        pl.semaphore_signal(barrier, inc=1, device_id={"band": lax.rem(band + i, NB)}, device_id_type=MESH)
        return carry

    lax.fori_loop(1, NP, greet_pw, 0)
    lax.fori_loop(1, NB, greet_band, 0)
    for k in NAMES:
        loads[k].start()

    due = {}
    gone = {}

    def send_pw(src, dst, k):
        due[k], gone[k] = dst, dst.at[pl.ds(0, NP - 1)]
        pltpu.make_async_copy(src.at[me], dst.at[me], rsem.at[k]).start()

        def one(i, carry):
            to = lax.rem(me + i, NP)
            pltpu.make_async_remote_copy(
                src.at[to], dst.at[me], ssem.at[k], rsem.at[k], device_id={"pw": to}, device_id_type=MESH
            ).start()
            return carry

        lax.fori_loop(1, NP, one, 0)

    def send_band(src, dst, whole, k):
        due[k], gone[k] = whole, whole.at[pl.ds(0, whole.shape[0] // NB * (NB - 1))]
        pltpu.make_async_copy(src(band), dst, rsem.at[k]).start()

        def one(i, carry):
            to = lax.rem(band + i, NB)
            pltpu.make_async_remote_copy(
                src(to), dst, ssem.at[k], rsem.at[k], device_id={"band": to}, device_id_type=MESH
            ).start()
            return carry

        lax.fori_loop(1, NB, one, 0)

    def arrive(k):
        ref = due.pop(k)
        pltpu.make_async_copy(ref, ref, rsem.at[k]).wait()

    def finish():
        for k, ref in gone.items():
            pltpu.make_async_copy(ref, ref, ssem.at[k]).wait()

    inputs[0].wait()
    for i in range(NPW_DEV // 128):
        slv[:, i * 128 : (i + 1) * 128] = slots[i : i + 1]
    slot = slv[...]
    stick = lax.shift_right_logical(slot, 7)
    zval = lax.bitwise_and(slot, 127)
    kzi = lax.bitwise_and(zval + 32, 127)
    sh[...] = (iota((128, NPW_DEV), 0) == stick).astype(BF16)

    def scatter(re, im):
        hit = iota((KZ, NPW_DEV), 0) == kzi
        for c, x in enumerate((re, im)):
            hi = x.astype(BF16).astype(F32)
            lo = x - hi
            cz[c * KZ : (c + 1) * KZ] = jnp.where(hit, hi, 0.0).astype(BF16)
            cz[(2 + c) * KZ : (3 + c) * KZ] = jnp.where(hit, lo, 0.0).astype(BF16)
        g = mm_nt(cz[...], sh[...])
        g = g[: 2 * KZ] + g[2 * KZ :]
        return mm(table("z_up"), stack_rows(g)).reshape(NP, 8, 128)

    inputs[1].wait()
    sb1[0] = scatter(coeffs[0, 0:1], coeffs[1, 0:1])
    pl.semaphore_wait(barrier, NP - 1 + NB - 1)
    send_pw(sb1.at[0], rb1.at[0], A1)
    sb1[1] = scatter(coeffs[0, 1:2], coeffs[1, 1:2])
    send_pw(sb1.at[1], rb1.at[1], A1 + 1)

    inputs[2].wait()
    c0, c1, c2 = (cols[pl.ds(i, 8, stride=3), :] for i in range(3))
    lane8 = iota((8, 128), 1)
    blocks = (
        c0,
        jnp.where(lane8 < 32, pltpu.roll(c0, 32, 1), pltpu.roll(c1, 32, 1)),
        jnp.where(lane8 < 64, pltpu.roll(c1, 64, 1), pltpu.roll(c2, 64, 1)),
        pltpu.roll(c2, 96, 1),
    )
    for i, block in enumerate(blocks):
        cpad[pl.ds(i, 8, stride=4), :] = jnp.where(lane8 < ST, block, -1)
    c = cpad[...]
    xp = lax.bitwise_and(lax.shift_right_arithmetic(c, 7) + 32, 127)
    yp = lax.bitwise_and(c + 32, 127)
    edge = yp == 64
    r = jnp.where(edge, 16, lax.shift_right_logical(xp, 2))
    q = jnp.where(edge, 64, lax.bitwise_and(xp, 3) * 64 + yp)
    r = jnp.where(c < 0, -1, r)
    for p in range(NP):
        mt[:, p * 128 : (p + 1) * 128] = (iota((NR, 128), 0) == r[p : p + 1]).astype(F32)
        tt[:, p * 128 : (p + 1) * 128] = (iota((256, 128), 0) == q[p : p + 1]).astype(BF16)

    inputs[3].wait()
    inputs[4].wait()

    def to_field(rb):
        g = None
        for p0 in range(0, NP, 4):
            block = []
            for p in range(p0, p0 + 4):
                d = rb[p]
                m = mt[:, p * 128 : (p + 1) * 128]
                hi = d.astype(BF16).astype(F32)
                rows = [jnp.broadcast_to(v[i : i + 1], (NR, 128)) * m for v in (hi, d - hi) for i in range(8)]
                block.append(jnp.concatenate(rows, axis=0).astype(BF16))
            y = mm_nt(jnp.concatenate(block, axis=1), tt[:, p0 * 128 : (p0 + 4) * 128])
            g = y if g is None else g + y
        g = g[: 8 * NR] + g[8 * NR :]
        f = mm(stack_lanes(g), table("y_up"))
        re, im = [], []
        for z in range(4):
            a = f[(2 * z) * NR : (2 * z + 1) * NR]
            b = f[(2 * z + 1) * NR : (2 * z + 2) * NR]
            re.append(a[:, :512] - b[:, 512:])
            im.append(a[:, 512:] + b[:, :512])
        rows = [
            jnp.concatenate([x[z][:, j * 128 : (j + 1) * 128] for z in range(4)], axis=1)
            for x in (re, im)
            for j in range(4)
        ]
        return mm(table("x_up"), stack_rows(jnp.concatenate(rows, axis=0)))

    dens = None
    for n in range(2):
        arrive(A1 + n)
        f = to_field(rb1.at[n])
        field[n] = f
        term = (f[:128] * f[:128] + f[128:] * f[128:]) * (occ[n] * (1.0 / 16.0))
        dens = term if dens is None else dens + term

    def plane_x(x, name):
        flipped = jnp.concatenate([turned(x[:, z * 128 : (z + 1) * 128]) for z in range(4)], axis=1)
        return mm(table(name), stack_rows(jnp.concatenate([x, flipped], axis=0)))

    def plane_inverse(x, name):
        y = plane_x(x, name)
        return rows_to_lanes(mm(stack_lanes(lanes_to_rows(y)), table("piy")))

    means = []
    for z in range(4):
        means.append(total(dens[:, z * 128 : (z + 1) * 128]) * (1.0 / (NG * NG)))
    mean = jnp.concatenate([jnp.broadcast_to(m, (1, 128)) for m in means], axis=1)
    dens = dens - mean
    xb[...] = plane_x(rows_to_lanes(mm(stack_lanes(lanes_to_rows(dens)), table("py"))), "px")
    head = jnp.where(lax.bitwise_and(iota((8, 512), 1), 127) == 0, mean * float(NG * NG), 0.0)
    xb[0:8] = xb[0:8] + jnp.where(iota((8, 512), 0) == 0, head, 0.0)
    send_band(lambda to: xb.at[pl.ds(pl.multiple_of(16 * to, 16), 16)], rsb.at[band], rsb, RS)

    own = cpad[pl.ds(me, 1), :]
    wx = wrapped(lax.bitwise_and(lax.shift_right_arithmetic(own, 7), 127))
    wy = wrapped(lax.bitwise_and(own, 127))
    reach = wx * wx + wy * wy
    coarse = lax.shift_right_logical(reach, 5).astype(F32)
    fine = lax.bitwise_and(reach, 31).astype(F32)
    both = jnp.concatenate([jnp.broadcast_to(coarse, (8, 128)), jnp.broadcast_to(fine, (8, 128))], axis=0)
    picked = mm(both.astype(BF16), sh[...])
    wz = wrapped(zval)
    kin[...] = (123.4 / (NG * NG)) * (32.0 * picked[0:1] + picked[8:9] + (wz * wz).astype(F32))

    apad[...] = jnp.full((3, 1024), -1, jnp.int32)
    apad[:, : atoms.shape[1]] = atoms[...]

    def spots(row):
        hot = (iota((128, 1024), 0) == apad[row : row + 1]).astype(BF16)
        return mm(table("circ"), jnp.concatenate([hot, hot], axis=0))

    gz[...] = spots(2)
    gy_hi, gy_lo = split(spots(1))
    gx = spots(0) * FORM
    for z in range(4):
        gl = gx * gz[pl.ds(4 * me + z, 1), :]
        g_hi, g_lo = split(gl)
        vloc[:, z * 128 : (z + 1) * 128] = mm_nt(g_hi, gy_hi) + mm_nt(g_lo, gy_hi) + mm_nt(g_hi, gy_lo)

    row = iota((256, 128), 0)
    lane = iota((256, 128), 1)
    wkz = wrapped(lax.shift_right_logical(row, 1))
    kx = 16 * band + 2 * lax.div(me, 4) + lax.bitwise_and(row, 1)
    wkx = wrapped(kx)
    ky = lax.bitwise_and(lane, 63)
    q = wkz * wkz + wkx * wkx + ky * ky
    corner = jnp.logical_and(q == 0, lane == 64)
    q = jnp.where(corner, 4096, q).astype(F32)
    factor = jnp.where(q > 0.0, (HARTREE / NG**3) / jnp.maximum(q, 1.0), 0.0)

    arrive(RS)
    s = rsb[0]
    for i in range(1, NB):
        s = s + rsb[i]
    sbuf[...] = s
    for i in range(8):
        for z in range(4):
            tb[i, 2 * z : 2 * z + 2, :] = s[2 * i : 2 * i + 2, z * 128 : (z + 1) * 128]
    mine = lax.div(me, 4)
    pltpu.make_async_copy(tb.at[mine], rb2.at[me], rsem.at[A2]).start()

    def out_a2(i, carry):
        to = lax.rem(me + i, NP)
        pltpu.make_async_remote_copy(
            tb.at[lax.div(to, 4)], rb2.at[me], ssem.at[A2], rsem.at[A2], device_id={"pw": to}, device_id_type=MESH
        ).start()
        return carry

    lax.fori_loop(1, NP, out_a2, 0)
    due[A2], gone[A2] = rb2, rb2.at[pl.ds(0, NP - 1)]

    arrive(A2)
    x = rb2[...].reshape(256, 128)
    flat = jnp.logical_and(lane == 0, kx == 0)
    x = x - jnp.where(flat, jnp.sum(jnp.where(flat, x, 0.0), axis=0, keepdims=True) * (1.0 / NG), 0.0)
    x = mm(table("pz"), stack_rows(jnp.concatenate([x, turned(x)], axis=0))) * factor
    x = mm(table("piz"), stack_rows(jnp.concatenate([x, turned(x)], axis=0)))
    ub[...] = x.reshape(NP, 8, 128)
    low = lax.rem(me, 4)
    turn = band * 8 + mine
    place = pl.ds(pl.multiple_of(8 * turn, 8), 8)
    pltpu.make_async_copy(ub.at[me], rbv.at[place], rsem.at[A3]).start()

    def out_a3(i, carry):
        to = lax.rem(turn + i, 64)
        spot = 4 * lax.rem(to, 8) + low
        pltpu.make_async_remote_copy(
            ub.at[spot],
            rbv.at[place],
            ssem.at[A3],
            rsem.at[A3],
            device_id={"band": lax.div(to, 8), "pw": spot},
            device_id_type=MESH,
        ).start()
        return carry

    lax.fori_loop(1, 64, out_a3, 0)
    due[A3], gone[A3] = rbv, rbv.at[pl.ds(0, 8 * 63)]
    arrive(A3)
    vk = [
        jnp.concatenate([rbv[pl.ds(2 * z + k, 64, stride=8), :] for k in range(2)], axis=0) for z in range(4)
    ]
    pot[...] = plane_inverse(jnp.concatenate(vk, axis=1), "pixp") + vloc[...]

    lane1 = iota((8, 128), 1)
    weight = NPW / NG**3
    for n in range(2):
        f = field[n]
        v = pot[...]
        u = jnp.concatenate([v * f[:128], v * f[128:]], axis=0)
        nsq_part = total(coeffs[0, n : n + 1] * coeffs[0, n : n + 1] + coeffs[1, n : n + 1] * coeffs[1, n : n + 1])
        cross_part = weight * total(u[:128] * f[:128] + u[128:] * f[128:]) + total(
            kin[...]
            * (coeffs[0, n : n + 1] * coeffs[0, n : n + 1] + coeffs[1, n : n + 1] * coeffs[1, n : n + 1])
        )
        x = mm(table("x_down"), stack_rows(u))
        rows = [
            jnp.concatenate(
                [x[(c * 4 + j) * NR : (c * 4 + j + 1) * NR, z * 128 : (z + 1) * 128] for j in range(4)], axis=1
            )
            for z in range(4)
            for c in range(2)
        ]
        o = mm(stack_lanes(jnp.concatenate(rows, axis=0)), table("y_down"))
        rows = []
        for z in range(4):
            a = o[(2 * z) * NR : (2 * z + 1) * NR]
            b = o[(2 * z + 1) * NR : (2 * z + 2) * NR]
            rows.append(a[:, :256] + b[:, 256:])
            rows.append(b[:, :256] - a[:, 256:])
        hi, lo = split(jnp.concatenate(rows, axis=0))
        hilo = jnp.concatenate([hi, lo], axis=1)
        extra = jnp.where(lane1 == 96, nsq_part, 0.0) + jnp.where(lane1 == 97, cross_part, 0.0)

        hot = tt[...]
        y = mm(hilo, jnp.concatenate([hot, hot], axis=0))
        m = mt[...]
        y = jnp.concatenate(
            [jnp.sum(y[k * NR : (k + 1) * NR] * m, axis=0, keepdims=True) for k in range(8)], axis=0
        )
        for p in range(NP):
            sb4[n, p] = y[:, p * 128 : (p + 1) * 128] + extra
        send_pw(sb4.at[n], rb4.at[n], A4 + n)

    at_band = pl.ds(pl.multiple_of(16 * band, 16), 16)
    send_band(lambda to: sbuf, dk.at[at_band], dk, AGD)

    states = []
    for n in range(2):
        arrive(A4 + n)
        r = rb4[n]
        ends = jnp.sum(r, axis=0)[0:1]
        nsq = jnp.sum(jnp.where(iota((1, 128), 1) == 96, ends, 0.0), axis=1, keepdims=True) + EPSILON
        cross = jnp.sum(jnp.where(iota((1, 128), 1) == 97, ends, 0.0), axis=1, keepdims=True)
        alpha0 = cross / nsq
        g = mm(table("z_down"), stack_rows(r.reshape(256, 128)))
        hi, lo = split(g)
        hilo = jnp.concatenate([hi, lo], axis=1)

        hot = sh[...]
        y = mm(hilo, jnp.concatenate([hot, hot], axis=0))
        pick = iota((KZ, NPW_DEV), 0) == lax.bitwise_and(slv[...] + 32, 127)
        for c in range(2):
            part = jnp.sum(jnp.where(pick, y[c * KZ : (c + 1) * KZ], 0.0), axis=0, keepdims=True)
            wvec[n, c : c + 1] = part + (kin[...] - alpha0) * coeffs[c, n : n + 1]
        w_re = wvec[n, 0:1]
        w_im = wvec[n, 1:2]
        sb5[n] = scatter(w_re, w_im)
        send_pw(sb5.at[n], rb5.at[n], A5 + n)
        wsq = w_re * w_re + w_im * w_im
        states.append((nsq, alpha0, total(wsq), total(wsq * kin[...])))

    out = jnp.zeros((8, 128), F32)
    for n in range(2):
        arrive(A5 + n)
        f = to_field(rb5.at[n])
        energy = weight * total(pot[...] * (f[:128] * f[:128] + f[128:] * f[128:])) + states[n][3]
        out = out + jnp.where(lane1 == 2 * n, states[n][2], 0.0) + jnp.where(lane1 == 2 * n + 1, energy, 0.0)
    sbr[...] = out
    pltpu.make_async_copy(sbr, rbr.at[me], rsem.at[AR]).start()

    def out_ar(i, carry):
        to = lax.rem(me + i, NP)
        pltpu.make_async_remote_copy(
            sbr, rbr.at[me], ssem.at[AR], rsem.at[AR], device_id={"pw": to}, device_id_type=MESH
        ).start()
        return carry

    lax.fori_loop(1, NP, out_ar, 0)
    due[AR], gone[AR] = rbr, rbr.at[pl.ds(0, NP - 1)]
    arrive(AGD)
    d = plane_inverse(dk[...], "pix") * (1.0 / (NG * NG))
    for z in range(4):
        dens_val[z] = d[:, z * 128 : (z + 1) * 128]
    dens_copy = pltpu.make_async_copy(dens_val, dens_out, osem.at[0])
    dens_copy.start()
    arrive(AR)
    ends = jnp.sum(rbr[...], axis=0)[0:1]
    for n in range(2):
        nsq, alpha0 = states[n][0], states[n][1]
        ww = jnp.sum(jnp.where(iota((1, 128), 1) == 2 * n, ends, 0.0), axis=1, keepdims=True)
        ew = jnp.sum(jnp.where(iota((1, 128), 1) == 2 * n + 1, ends, 0.0), axis=1, keepdims=True)
        spread_sq = ww / nsq + EPSILON
        spread = jnp.sqrt(spread_sq)
        alpha1 = ew / (nsq * spread_sq)
        first, second = exponential_weights(alpha0, alpha1, spread)
        sec_re = second[0] / spread
        sec_im = second[1] / spread
        c_re, c_im = coeffs[0, n : n + 1], coeffs[1, n : n + 1]
        w_re, w_im = wvec[n, 0:1], wvec[n, 1:2]
        new[0, n : n + 1] = first[0] * c_re - first[1] * c_im + (sec_re * w_re - sec_im * w_im)
        new[1, n : n + 1] = first[0] * c_im + first[1] * c_re + (sec_re * w_im + sec_im * w_re)

    new_copy = pltpu.make_async_copy(new, new_out, osem.at[1])
    new_copy.start()
    finish()
    dens_copy.wait()
    new_copy.wait()


def copies(new_in, dens_in, new_out, dens_out):
    new_out[...] = new_in[...]
    dens_out[...] = dens_in[...]


def local(coeffs, occupation, stick_columns, sphere_slots, atom_sites):
    cols = stick_columns.reshape(NP * ST // 128, 128)
    slots = sphere_slots.reshape(NPW_DEV // 128, 128)
    hbm = pl.BlockSpec(memory_space=pl.ANY)
    vm = pl.BlockSpec(memory_space=pltpu.VMEM)
    tables = [jnp.asarray(TABLES[k]) for k in NAMES]
    V = pltpu.VMEM
    results = (
        jax.ShapeDtypeStruct((2, 2, NPW_DEV), F32),
        jax.ShapeDtypeStruct((4, NG, NG), F32),
    )
    step = pl.pallas_call(
        kernel,
        out_shape=results,
        in_specs=[hbm] * (5 + len(NAMES)),
        out_specs=(hbm, hbm),
        scratch_shapes=[
            V((2, 2, NPW_DEV), F32),
            pltpu.SMEM((2,), F32),
            V((NP * ST // 128, 128), jnp.int32),
            V((NPW_DEV // 128, 128), jnp.int32),
            V(atom_sites.shape, jnp.int32),
            V((2, 2, NPW_DEV), F32),
            V((4, NG, NG), F32),
            V((128, NPW_DEV), BF16),
            V((4 * KZ, NPW_DEV), BF16),
            V((1, NPW_DEV), F32),
            V((256, 4096), BF16),
            V((NR, 4096), F32),
            V((2, 256, 512), F32),
            V((1, NPW_DEV), jnp.int32),
            V((NP, 128), jnp.int32),
            V((3, 1024), jnp.int32),
            V((128, 512), F32),
            V((128, 512), F32),
            V((2, 2, NPW_DEV), F32),
            V((2, NP, 8, 128), F32),
            V((2, NP, 8, 128), F32),
            V((128, 512), F32),
            V((NB, 16, 512), F32),
            V((16, 512), F32),
            V((8, 8, 128), F32),
            V((NP, 8, 128), F32),
            V((NP, 8, 128), F32),
            V((512, 128), F32),
            V((128, 512), F32),
            V((2, NP, 8, 128), F32),
            V((2, NP, 8, 128), F32),
            V((2, NP, 8, 128), F32),
            V((2, NP, 8, 128), F32),
            V((8, 128), F32),
            V((NP, 8, 128), F32),
            V((128, 1024), F32),
            pltpu.SemaphoreType.DMA((N_SEM,)),
            pltpu.SemaphoreType.DMA((N_SEM,)),
            pltpu.SemaphoreType.DMA((5,)),
            pltpu.SemaphoreType.DMA((2,)),
        ]
        + [V(TABLES[k].shape, BF16) for k in NAMES]
        + [pltpu.SemaphoreType.DMA((len(NAMES),))],
        compiler_params=pltpu.CompilerParams(
            collective_id=0, has_side_effects=True, vmem_limit_bytes=60 * 1024 * 1024
        ),
        name="step",
    )(coeffs, occupation, cols, slots, atom_sites, *tables)
    return pl.pallas_call(
        copies,
        out_shape=results,
        in_specs=[vm, vm],
        out_specs=(vm, vm),
        name="results",
    )(*step)


def solution(mesh):
    in_specs = (P(None, "band", "pw"), P("band"), P(), P("pw"), P())
    out_specs = (P(None, "band", "pw"), P("pw", None, None))
    return jax.shard_map(local, mesh=mesh, in_specs=in_specs, out_specs=out_specs, check_vma=False)
```

time: 680 us -> 78.5 us (0.12)
  matrix products: 230 us -> 0 us
  blocking collectives: 214 us -> 0 us
  waiting for transfers between devices: 82.5 us -> 0 us
  Pallas kernels: 0 us -> 77.7 us
  local copies, waits for them, and re-layouts: 77 us -> 0 us
  starting transfers between devices: 32.5 us -> 0 us
  between operations: 15.1 us -> 0.64 us
  loops' own time: 13.3 us -> 0 us
  other arithmetic: 9.44 us -> 0 us
    dot_general x134 -> x0, matrix products: 230 us -> none  [product(): return jnp.einsum(pattern, first, second, precision=HIGHEST)]
    psum x3 -> x0, blocking collectives: 189 us -> none  [the longest x1 64.7 us: local(): lax.psum(jnp.sum(rest_re * rest_re + rest_im * rest_im, axis=1), 'pw')]
    pallas_call x0 -> x2, Pallas kernels: none -> 77.7 us  [the longest x1 76 us: local(): pl.pallas_call(kernel, out_shape=results, in_specs=[hbm] * (5 + len(NAMES...]
    psum x1 -> x0, waiting for transfers between devices: 63.1 us -> none  [local(): density_total = lax.psum(partial_density, 'band')]
    unnamed x32 -> x0, local copies, waits for them, and re-layouts: 42.7 us -> none
    all_to_all x4 -> x0, starting transfers between devices: 32.1 us -> none  [the longest x1 12.2 us: local(): lax.all_to_all(jnp.stack(mixed), 'pw', split_axis=2, concat_axis=1, tiled...]
    all_to_all x2 -> x0, blocking collectives: 24.4 us -> none  [the longest x1 12.4 us: local(): lax.all_to_all(sticks_of(next_re, next_im), 'pw', split_axis=2, concat_ax...]
    all_to_all x4 -> x0, waiting for transfers between devices: 19.4 us -> none  [the longest x1 11.2 us: local(): lax.all_to_all(jnp.stack(back_depth), 'pw', split_axis=1, concat_axis=2,...]
  transfers between devices with their start and end apart: 5 -> 0, of which waited for: 3 -> 0; matrix products, arithmetic and copies ran while one was open for 4% -> 0% of each run, Pallas kernels for 0% -> 0%
where the time goes in v1:
time: 78.5 us; the launch traced here: 78.4 us
  Pallas kernels  77.7 us (99%)
    pallas_call x1, Pallas kernels, local(): pl.pallas_call(kernel, out_shape=results, in_specs=[hbm] * (5 + len(NAMES...  76 us
    pallas_call x1, Pallas kernels, local(): pl.pallas_call(copies, out_shape=results, in_specs=[vm, vm], out_specs=(v...  1.71 us

profile of v1, /device:TPU:1, one launch (start us, length us, event | category | flops | bytes accessed | tf_op | source)
XLA Modules:
  0.0 78.4 jit_solution(5149778243894298010)
XLA Ops:
  0.6 76.0 %step.1 = (f32[2,2,3584]{2,1,0:T(2,128)}, f32[4,128,128]{2,1,0:T(8,128)}) custom-call(f32[2,2,3584]{2,1,0:T(2,128)} %coeffs_in.1, f32[2]{0:T(128)} %occ_in.1, s32[24,128]{1,0:T(8,128)} %bitcast.3, s32[28,128]{1,0:T(8,128)} %bitcast.2, s32[3,1000]{1,0:T(4,128)} %atoms_in.1, bf16[256,480]{1,0:T(8,128)(2,1)} %constant.28.clone.refs_0_, ...), custom_call_target="tpu_custom_call" | custom-call | tf_op jit(solution)/shard_map/step/pallas_call | solution.py:599
  76.7 1.7 %results.1 = (f32[2,2,3584]{2,1,0:T(2,128)}, f32[4,128,128]{2,1,0:T(8,128)}) custom-call(f32[2,2,3584]{2,1,0:T(2,128)} %get-tuple-element.4.new_in, f32[4,128,128]{2,1,0:T(8,128)} %get-tuple-element.5.dens_in), custom_call_target="tpu_custom_call" | custom-call | tf_op jit(solution)/shard_map/results/pallas_call | solution.py:653

commit v2 on v1

--- a/solution.py
+++ b/solution.py
@@ -20,8 +20,9 @@
 NPW_DEV = 3584
 NPW = NPW_DEV * NP
 ST = 96
-KZ = 80
-NR = 24
+KH = 40
+NR = 16
+NX = 8 * NR + 16
 TIME_STEP = 0.2
 EPSILON = 1e-06
 STEP = 2.0 * math.pi / NG
@@ -33,6 +34,8 @@
 
 A1, RS, A2, A3, AGV, AGD, A4, A5, AR = 0, 2, 3, 4, 5, 6, 7, 9, 11
 N_SEM = 12
+MIX = 13
+FAR_FIRST = (4, 3, 5, 2, 6, 1, 7)
 
 
 def parts(x):
@@ -58,45 +61,38 @@
 
 def build_tables():
     grid = np.arange(NG)
-    kz_mask = (np.arange(KZ) <= 64).astype(np.float64)
-    kz = np.arange(KZ) - 32
     tables = {}
-    c, s = phases(grid, kz)
-    c, s = c * kz_mask, s * kz_mask
-    up = np.zeros((NG, 2, 2, KZ))
-    up[:, 0, 0], up[:, 0, 1], up[:, 1, 0], up[:, 1, 1] = c, -s, s, c
-    tables["z_up"] = left_table(up.reshape(2 * NG, 2 * KZ))
-    down = np.zeros((2, KZ, NG, 2))
-    down[0, :, :, 0], down[0, :, :, 1] = c.T, s.T
-    down[1, :, :, 0], down[1, :, :, 1] = -s.T, c.T
-    tables["z_down"] = left_table(down.reshape(2 * KZ, 2 * NG))
-
-    wy = np.tile(np.arange(64) - 32, (4, 1))
-    wy[1, 0] = 32
-    y_up = np.zeros((4, 64, 2, 4, NG))
-    y_down = np.zeros((4, NG, 2, 4, 64))
-    for j in range(4):
-        c, s = phases(wy[j], grid)
-        y_up[j, :, 0, j], y_up[j, :, 1, j] = c, s
+    kz = 2 * np.arange(KH)[None, :] + np.arange(2)[:, None]
+    valid = (kz <= 64).reshape(-1).astype(np.float64)
+    c, s = phases(grid, kz.reshape(-1) - 32)
+    c, s = (c * valid).reshape(NG, 2, KH), (s * valid).reshape(NG, 2, KH)
+    up = np.zeros((NG, 2, 2, 2, KH))
+    up[:, 0, :, 0], up[:, 0, :, 1], up[:, 1, :, 0], up[:, 1, :, 1] = c, -s, s, c
+    tables["z_up"] = left_table(up.reshape(2 * NG, 4 * KH))
+    down = np.zeros((NG, 2, 2, 2, KH))
+    down[:, 0, :, 0], down[:, 1, :, 0], down[:, 0, :, 1], down[:, 1, :, 1] = c, s, -s, c
+    tables["z_down"] = left_table(down.reshape(2 * NG, 4 * KH).T)
+
+    c, s = phases(np.arange(64) - 32, grid)
+    hi, lo = parts(np.concatenate([c, s], axis=1))
+    none = np.zeros_like(lo)
+    tables["y_even"] = np.concatenate([hi, hi, lo, none])
+    tables["y_odd"] = np.concatenate([hi, hi, none, lo])
+    y_down = np.zeros((2, NG, 2, 2, 64))
+    for j in range(2):
         y_down[j, :, 0, j], y_down[j, :, 1, j] = c.T, s.T
-    tables["y_up"] = right_table(y_up.reshape(256, 1024))
-    tables["y_down"] = right_table(y_down.reshape(512, 512))
-
-    wx = np.zeros((4, NR))
-    xm = np.zeros((4, NR))
-    for j in range(4):
-        for r in range(16):
-            wx[j, r], xm[j, r] = 4 * r + j - 32, 1.0
-    wx[0, 16], xm[0, 16] = 32, 1.0
-    wx[1, 16], xm[1, 16] = 0, 1.0
+    tables["y_down"] = right_table(y_down.reshape(256, 256))
+
+    wx = 4 * np.arange(NR)[None, :] + np.arange(4)[:, None] - 32
     c, s = phases(grid, wx.reshape(-1))
-    c, s = c * xm.reshape(-1), s * xm.reshape(-1)
-    x_up = np.zeros((2, NG, 2, 4 * NR))
-    x_up[0, :, 0], x_up[0, :, 1], x_up[1, :, 0], x_up[1, :, 1] = c, -s, s, c
-    tables["x_up"] = left_table(TO_GRID * x_up.reshape(2 * NG, 8 * NR))
-    x_down = np.zeros((2, 4 * NR, 2, NG))
-    x_down[0, :, 0], x_down[0, :, 1], x_down[1, :, 0], x_down[1, :, 1] = c.T, s.T, -s.T, c.T
-    tables["x_down"] = left_table(TO_SPHERE * x_down.reshape(8 * NR, 2 * NG))
+    x_up = np.zeros((2, NG, NX))
+    x_up[:, :, : 8 * NR] = np.stack([np.concatenate([c, -s], axis=1), np.concatenate([s, c], axis=1)])
+    for first, w in ((8 * NR, 32), (8 * NR + 2, 0)):
+        c, s = phases(grid, np.array([w]))
+        x_up[0, :, first], x_up[0, :, first + 1] = c[:, 0], -s[:, 0]
+        x_up[1, :, first], x_up[1, :, first + 1] = s[:, 0], c[:, 0]
+    tables["x_up"] = left_table(TO_GRID * x_up.reshape(2 * NG, NX))
+    tables["x_down"] = left_table(TO_SPHERE * x_up.reshape(2 * NG, NX).T)
 
     c, s = phases(grid, np.arange(64))
     fwd = np.zeros((NG, 2, 64))
@@ -113,10 +109,9 @@
     tables["pix"] = left_table(np.concatenate([c, -s], axis=1))
     pairs = np.concatenate([grid[0::2], grid[1::2]])
     tables["pixp"] = left_table(np.concatenate([c[:, pairs], -s[:, pairs]], axis=1))
-    pair = np.eye(2)
-    cc, ss = np.kron(c, pair), np.kron(s, pair)
-    tables["pz"] = left_table(np.concatenate([cc, ss], axis=1))
-    tables["piz"] = left_table(np.concatenate([cc, -ss], axis=1))
+    order = (4 * np.arange(NP)[None, :] + np.arange(4)[:, None]).reshape(-1)
+    tables["pz"] = left_table(np.concatenate([c[:, order], s[:, order]], axis=1))
+    tables["piz"] = left_table(np.concatenate([c[order], -s[order]], axis=1))
 
     wk = np.where(grid < 64, grid, grid - NG)
     gauss = np.exp(-(wk**2) / (2.0 * WIDTH * WIDTH))
@@ -127,7 +122,7 @@
 
 
 TABLES = build_tables()
-NAMES = ("z_up", "y_up", "x_up", "py", "px", "circ", "pz", "piz", "pixp", "piy", "x_down", "y_down", "z_down", "pix")
+NAMES = ("z_up", "y_even", "y_odd", "x_up", "py", "px", "circ", "pz", "piz", "pixp", "piy", "x_down", "y_down", "z_down", "pix")
 
 
 def mm(a, b):
@@ -167,7 +162,8 @@
 
 def turned(x):
     sgn = jnp.where(iota((1, 128), 1) < 64, 1.0, -1.0).astype(F32)
-    return pltpu.roll(x, 64, 1) * sgn
+    blocks = [pltpu.roll(x[:, i : i + 128], 64, 1) * sgn for i in range(0, x.shape[1], 128)]
+    return jnp.concatenate(blocks, axis=1)
 
 
 def lanes_to_rows(x):
@@ -200,7 +196,7 @@
     t = dict(zip(NAMES, refs[: len(NAMES)]))
     held = dict(zip(NAMES, refs[-len(NAMES) - 1 : -1]))
     tsem = refs[-1]
-    (new_out, dens_out, coeffs, occ, cols, slots, atoms, new, dens_val, sh, cz, kin, tt, mt, field, slv, cpad, apad, vloc, pot, wvec, sb1, rb1, xb, rsb, sbuf, tb, rb2,
+    (new_out, dens_out, coeffs, occ, cols, slots, atoms, new, dens_val, sh, sht, cz, kin, tt, mt, ms, field, slv, cpad, apad, vloc, pot, wvec, sb1, rb1, xb, rsb, sbuf, tb, rb2,
      ub, rbv, dk, sb4, rb4, sb5, rb5, sbr, rbr, gz, ssem, rsem, isem, osem) = refs[len(NAMES) : -len(NAMES) - 1]
     me = lax.axis_index("pw")
     band = lax.axis_index("band")
@@ -239,7 +235,7 @@
         pltpu.make_async_copy(src.at[me], dst.at[me], rsem.at[k]).start()
 
         def one(i, carry):
-            to = lax.rem(me + i, NP)
+            to = lax.rem(me + MIX * i, NP)
             pltpu.make_async_remote_copy(
                 src.at[to], dst.at[me], ssem.at[k], rsem.at[k], device_id={"pw": to}, device_id_type=MESH
             ).start()
@@ -251,14 +247,11 @@
         due[k], gone[k] = whole, whole.at[pl.ds(0, whole.shape[0] // NB * (NB - 1))]
         pltpu.make_async_copy(src(band), dst, rsem.at[k]).start()
 
-        def one(i, carry):
+        for i in FAR_FIRST:
             to = lax.rem(band + i, NB)
             pltpu.make_async_remote_copy(
                 src(to), dst, ssem.at[k], rsem.at[k], device_id={"band": to}, device_id_type=MESH
             ).start()
-            return carry
-
-        lax.fori_loop(1, NB, one, 0)
 
     def arrive(k):
         ref = due.pop(k)
@@ -275,24 +268,26 @@
     stick = lax.shift_right_logical(slot, 7)
     zval = lax.bitwise_and(slot, 127)
     kzi = lax.bitwise_and(zval + 32, 127)
-    sh[...] = (iota((128, NPW_DEV), 0) == stick).astype(BF16)
-
-    def scatter(re, im):
-        hit = iota((KZ, NPW_DEV), 0) == kzi
-        for c, x in enumerate((re, im)):
-            hi = x.astype(BF16).astype(F32)
-            lo = x - hi
-            cz[c * KZ : (c + 1) * KZ] = jnp.where(hit, hi, 0.0).astype(BF16)
-            cz[(2 + c) * KZ : (3 + c) * KZ] = jnp.where(hit, lo, 0.0).astype(BF16)
-        g = mm_nt(cz[...], sh[...])
-        g = g[: 2 * KZ] + g[2 * KZ :]
+    khi = lax.shift_right_logical(kzi, 1)
+    sh[...] = (iota((256, NPW_DEV), 0) == lax.bitwise_and(kzi, 1) * 128 + stick).astype(BF16)
+
+    def scatter(re, im, late):
+        hit = iota((KH, NPW_DEV), 0) == khi
+        re_hi = re.astype(BF16).astype(F32)
+        im_hi = im.astype(BF16).astype(F32)
+        for k, pair in enumerate(((re_hi, im_hi), (re - re_hi, im - im_hi))):
+            rows = jnp.concatenate([jnp.where(hit, x, 0.0) for x in pair], axis=0)
+            cz[k * 2 * KH : (k + 1) * 2 * KH] = rows.astype(BF16)
+        g = mm(cz[...], sht[...]) if late else mm_nt(cz[...], sh[...])
+        g = g[: 2 * KH] + g[2 * KH :]
+        g = jnp.concatenate([g[:, :128], g[:, 128:]], axis=0)
         return mm(table("z_up"), stack_rows(g)).reshape(NP, 8, 128)
 
     inputs[1].wait()
-    sb1[0] = scatter(coeffs[0, 0:1], coeffs[1, 0:1])
+    sb1[0] = scatter(coeffs[0, 0:1], coeffs[1, 0:1], False)
     pl.semaphore_wait(barrier, NP - 1 + NB - 1)
     send_pw(sb1.at[0], rb1.at[0], A1)
-    sb1[1] = scatter(coeffs[0, 1:2], coeffs[1, 1:2])
+    sb1[1] = scatter(coeffs[0, 1:2], coeffs[1, 1:2], False)
     send_pw(sb1.at[1], rb1.at[1], A1 + 1)
 
     inputs[2].wait()
@@ -309,42 +304,68 @@
     c = cpad[...]
     xp = lax.bitwise_and(lax.shift_right_arithmetic(c, 7) + 32, 127)
     yp = lax.bitwise_and(c + 32, 127)
-    edge = yp == 64
-    r = jnp.where(edge, 16, lax.shift_right_logical(xp, 2))
-    q = jnp.where(edge, 64, lax.bitwise_and(xp, 3) * 64 + yp)
-    r = jnp.where(c < 0, -1, r)
+    far_x = jnp.logical_and(c >= 0, xp == 64)
+    far_y = jnp.logical_and(c >= 0, yp == 64)
+    regular = jnp.logical_and(c >= 0, jnp.logical_and(xp < 64, yp < 64))
+    r = jnp.where(regular, lax.shift_right_logical(xp, 2), -1)
+    q = lax.bitwise_and(xp, 3) * 64 + yp
     for p in range(NP):
-        mt[:, p * 128 : (p + 1) * 128] = (iota((NR, 128), 0) == r[p : p + 1]).astype(F32)
-        tt[:, p * 128 : (p + 1) * 128] = (iota((256, 128), 0) == q[p : p + 1]).astype(BF16)
+        at = slice(p * 128, (p + 1) * 128)
+        mt[:, at] = (iota((NR, 128), 0) == r[p : p + 1]).astype(F32)
+        tt[:, at] = (iota((256, 128), 0) == q[p : p + 1]).astype(BF16)
+        ms[0:1, at] = far_x[p : p + 1].astype(F32)
+        ms[1:2, at] = far_y[p : p + 1].astype(F32)
 
     inputs[3].wait()
     inputs[4].wait()
 
+    quarter = lax.bitwise_and(iota((1, 128), 1), 3)
+    cos_b = jnp.where(quarter == 0, 1.0, jnp.where(quarter == 2, -1.0, 0.0))
+    sin_b = jnp.where(quarter == 1, 1.0, jnp.where(quarter == 3, -1.0, 0.0))
+
     def to_field(rb):
         g = None
+        ends = [jnp.zeros((8, 128), F32), jnp.zeros((8, 128), F32)]
         for p0 in range(0, NP, 4):
             block = []
             for p in range(p0, p0 + 4):
                 d = rb[p]
                 m = mt[:, p * 128 : (p + 1) * 128]
+                ends = [x + d * ms[i : i + 1, p * 128 : (p + 1) * 128] for i, x in enumerate(ends)]
                 hi = d.astype(BF16).astype(F32)
                 rows = [jnp.broadcast_to(v[i : i + 1], (NR, 128)) * m for v in (hi, d - hi) for i in range(8)]
                 block.append(jnp.concatenate(rows, axis=0).astype(BF16))
             y = mm_nt(jnp.concatenate(block, axis=1), tt[:, p0 * 128 : (p0 + 4) * 128])
             g = y if g is None else g + y
         g = g[: 8 * NR] + g[8 * NR :]
-        f = mm(stack_lanes(g), table("y_up"))
+        hi = g.astype(BF16).astype(F32)
+        lo = g - hi
+        left = iota((1, 128), 1) < 64
         re, im = [], []
+        for j in range(4):
+            at = slice(j // 2 * 128, j // 2 * 128 + 128)
+            h, l = hi[:, at], pltpu.roll(lo[:, at], 64, 1)
+            both = jnp.where(left, h, l) if j % 2 == 0 else jnp.where(left, l, h)
+            f = jnp.concatenate([both, h], axis=1).astype(BF16)
+            f = mm(f, table("y_even" if j % 2 == 0 else "y_odd"))
+            row_re, row_im = [], []
+            for z in range(4):
+                a = f[(2 * z) * NR : (2 * z + 1) * NR]
+                b = f[(2 * z + 1) * NR : (2 * z + 2) * NR]
+                row_re.append(a[:, :128] - b[:, 128:])
+                row_im.append(a[:, 128:] + b[:, :128])
+            re.append(jnp.concatenate(row_re, axis=1))
+            im.append(jnp.concatenate(row_im, axis=1))
+        rows = re + im
+        ex, ey = (jnp.sum(x, axis=1, keepdims=True) for x in ends)
+        extra = []
         for z in range(4):
-            a = f[(2 * z) * NR : (2 * z + 1) * NR]
-            b = f[(2 * z + 1) * NR : (2 * z + 2) * NR]
-            re.append(a[:, :512] - b[:, 512:])
-            im.append(a[:, 512:] + b[:, :512])
-        rows = [
-            jnp.concatenate([x[z][:, j * 128 : (j + 1) * 128] for z in range(4)], axis=1)
-            for x in (re, im)
-            for j in range(4)
-        ]
+            k = 2 * z
+            yr, yi = ey[k : k + 1], ey[k + 1 : k + 2]
+            x = jnp.broadcast_to(ex[k : k + 2], (2, 128))
+            y = [yr * cos_b - yi * sin_b, yr * sin_b + yi * cos_b]
+            extra.append(jnp.concatenate([x] + y + [jnp.zeros((12, 128), F32)], axis=0))
+        rows.append(jnp.concatenate(extra, axis=1))
         return mm(table("x_up"), stack_rows(jnp.concatenate(rows, axis=0)))
 
     dens = None
@@ -380,7 +401,7 @@
     coarse = lax.shift_right_logical(reach, 5).astype(F32)
     fine = lax.bitwise_and(reach, 31).astype(F32)
     both = jnp.concatenate([jnp.broadcast_to(coarse, (8, 128)), jnp.broadcast_to(fine, (8, 128))], axis=0)
-    picked = mm(both.astype(BF16), sh[...])
+    picked = mm(jnp.concatenate([both, both], axis=1).astype(BF16), sh[...])
     wz = wrapped(zval)
     kin[...] = (123.4 / (NG * NG)) * (32.0 * picked[0:1] + picked[8:9] + (wz * wz).astype(F32))
 
@@ -399,10 +420,10 @@
         g_hi, g_lo = split(gl)
         vloc[:, z * 128 : (z + 1) * 128] = mm_nt(g_hi, gy_hi) + mm_nt(g_lo, gy_hi) + mm_nt(g_hi, gy_lo)
 
-    row = iota((256, 128), 0)
-    lane = iota((256, 128), 1)
-    wkz = wrapped(lax.shift_right_logical(row, 1))
-    kx = 16 * band + 2 * lax.div(me, 4) + lax.bitwise_and(row, 1)
+    lane = iota((128, 256), 1)
+    wkz = wrapped(iota((128, 256), 0))
+    kx = 16 * band + 2 * lax.div(me, 4) + lax.shift_right_logical(lane, 7)
+    lane = lax.bitwise_and(lane, 127)
     wkx = wrapped(kx)
     ky = lax.bitwise_and(lane, 63)
     q = wkz * wkz + wkx * wkx + ky * ky
@@ -410,6 +431,12 @@
     q = jnp.where(corner, 4096, q).astype(F32)
     factor = jnp.where(q > 0.0, (HARTREE / NG**3) / jnp.maximum(q, 1.0), 0.0)
 
+    def transpose(i, carry):
+        at = pl.ds(pl.multiple_of(i * 512, 512), 512)
+        sht[at, :] = sh[:, at].T
+        return carry
+
+    lax.fori_loop(0, NPW_DEV // 512, transpose, 0)
     arrive(RS)
     s = rsb[0]
     for i in range(1, NB):
@@ -419,44 +446,58 @@
         for z in range(4):
             tb[i, 2 * z : 2 * z + 2, :] = s[2 * i : 2 * i + 2, z * 128 : (z + 1) * 128]
     mine = lax.div(me, 4)
-    pltpu.make_async_copy(tb.at[mine], rb2.at[me], rsem.at[A2]).start()
+    slot_me = pl.ds(pl.multiple_of(8 * me, 8), 8)
+    pltpu.make_async_copy(tb.at[mine], rb2.at[slot_me], rsem.at[A2]).start()
 
     def out_a2(i, carry):
-        to = lax.rem(me + i, NP)
+        to = lax.rem(me + MIX * i, NP)
         pltpu.make_async_remote_copy(
-            tb.at[lax.div(to, 4)], rb2.at[me], ssem.at[A2], rsem.at[A2], device_id={"pw": to}, device_id_type=MESH
+            tb.at[lax.div(to, 4)], rb2.at[slot_me], ssem.at[A2], rsem.at[A2], device_id={"pw": to}, device_id_type=MESH
         ).start()
         return carry
 
     lax.fori_loop(1, NP, out_a2, 0)
-    due[A2], gone[A2] = rb2, rb2.at[pl.ds(0, NP - 1)]
+    due[A2], gone[A2] = rb2, rb2.at[pl.ds(0, 8 * (NP - 1))]
 
     arrive(A2)
-    x = rb2[...].reshape(256, 128)
+    x = [
+        jnp.concatenate([rb2[pl.ds(2 * z + k, NP, stride=8), :] for z in range(4)], axis=0) for k in range(2)
+    ]
+    x = jnp.concatenate(x, axis=1)
     flat = jnp.logical_and(lane == 0, kx == 0)
     x = x - jnp.where(flat, jnp.sum(jnp.where(flat, x, 0.0), axis=0, keepdims=True) * (1.0 / NG), 0.0)
     x = mm(table("pz"), stack_rows(jnp.concatenate([x, turned(x)], axis=0))) * factor
     x = mm(table("piz"), stack_rows(jnp.concatenate([x, turned(x)], axis=0)))
-    ub[...] = x.reshape(NP, 8, 128)
+    for z in range(4):
+        for k in range(2):
+            ub[pl.ds(2 * z + k, NP, stride=8), :] = x[z * NP : (z + 1) * NP, k * 128 : (k + 1) * 128]
     low = lax.rem(me, 4)
     turn = band * 8 + mine
     place = pl.ds(pl.multiple_of(8 * turn, 8), 8)
-    pltpu.make_async_copy(ub.at[me], rbv.at[place], rsem.at[A3]).start()
-
-    def out_a3(i, carry):
-        to = lax.rem(turn + i, 64)
-        spot = 4 * lax.rem(to, 8) + low
-        pltpu.make_async_remote_copy(
-            ub.at[spot],
-            rbv.at[place],
-            ssem.at[A3],
-            rsem.at[A3],
-            device_id={"band": lax.div(to, 8), "pw": spot},
-            device_id_type=MESH,
-        ).start()
+    pltpu.make_async_copy(ub.at[slot_me], rbv.at[place], rsem.at[A3]).start()
+
+    def out_a3(i, offsets):
+        spot = 4 * lax.rem(mine + i, 8) + low
+        for offset in offsets:
+            pltpu.make_async_remote_copy(
+                ub.at[pl.ds(pl.multiple_of(8 * spot, 8), 8)],
+                rbv.at[place],
+                ssem.at[A3],
+                rsem.at[A3],
+                device_id={"band": lax.rem(band + offset, NB), "pw": spot},
+                device_id_type=MESH,
+            ).start()
+
+    def out_far(i, carry):
+        out_a3(i, FAR_FIRST)
         return carry
 
-    lax.fori_loop(1, 64, out_a3, 0)
+    def out_near(i, carry):
+        out_a3(i, (0,))
+        return carry
+
+    lax.fori_loop(0, 8, out_far, 0)
+    lax.fori_loop(1, 8, out_near, 0)
     due[A3], gone[A3] = rbv, rbv.at[pl.ds(0, 8 * 63)]
     arrive(A3)
     vk = [
@@ -476,30 +517,41 @@
             * (coeffs[0, n : n + 1] * coeffs[0, n : n + 1] + coeffs[1, n : n + 1] * coeffs[1, n : n + 1])
         )
         x = mm(table("x_down"), stack_rows(u))
-        rows = [
-            jnp.concatenate(
-                [x[(c * 4 + j) * NR : (c * 4 + j + 1) * NR, z * 128 : (z + 1) * 128] for j in range(4)], axis=1
-            )
-            for z in range(4)
-            for c in range(2)
-        ]
-        o = mm(stack_lanes(jnp.concatenate(rows, axis=0)), table("y_down"))
-        rows = []
+        tiles = []
+        for t in range(2):
+            rows = [
+                jnp.concatenate(
+                    [x[(c * 4 + j) * NR : (c * 4 + j + 1) * NR, z * 128 : (z + 1) * 128] for j in (2 * t, 2 * t + 1)],
+                    axis=1,
+                )
+                for z in range(4)
+                for c in range(2)
+            ]
+            o = mm(stack_lanes(jnp.concatenate(rows, axis=0)), table("y_down"))
+            rows = []
+            for z in range(4):
+                a = o[(2 * z) * NR : (2 * z + 1) * NR]
+                b = o[(2 * z + 1) * NR : (2 * z + 2) * NR]
+                rows.append(a[:, :128] + b[:, 128:])
+                rows.append(b[:, :128] - a[:, 128:])
+            tiles.append(jnp.concatenate(rows, axis=0))
+        hi, lo = split(jnp.concatenate(tiles, axis=1))
+        edge = x[8 * NR :]
+        ex, ey = [], []
         for z in range(4):
-            a = o[(2 * z) * NR : (2 * z + 1) * NR]
-            b = o[(2 * z + 1) * NR : (2 * z + 2) * NR]
-            rows.append(a[:, :256] + b[:, 256:])
-            rows.append(b[:, :256] - a[:, 256:])
-        hi, lo = split(jnp.concatenate(rows, axis=0))
-        hilo = jnp.concatenate([hi, lo], axis=1)
+            a, b, c, d = (edge[i : i + 1, z * 128 : (z + 1) * 128] for i in range(4))
+            ex += [a, b]
+            ey += [c * cos_b + d * sin_b, d * cos_b - c * sin_b]
+        ex, ey = (jnp.sum(jnp.concatenate(v, axis=0), axis=1, keepdims=True) for v in (ex, ey))
         extra = jnp.where(lane1 == 96, nsq_part, 0.0) + jnp.where(lane1 == 97, cross_part, 0.0)
 
-        hot = tt[...]
-        y = mm(hilo, jnp.concatenate([hot, hot], axis=0))
+        y = mm(jnp.concatenate([hi, lo], axis=0), tt[...])
+        y = y[: 8 * NR] + y[8 * NR :]
         m = mt[...]
         y = jnp.concatenate(
             [jnp.sum(y[k * NR : (k + 1) * NR] * m, axis=0, keepdims=True) for k in range(8)], axis=0
         )
+        y = y + ex * ms[0:1] + ey * ms[1:2]
         for p in range(NP):
             sb4[n, p] = y[:, p * 128 : (p + 1) * 128] + extra
         send_pw(sb4.at[n], rb4.at[n], A4 + n)
@@ -516,18 +568,16 @@
         cross = jnp.sum(jnp.where(iota((1, 128), 1) == 97, ends, 0.0), axis=1, keepdims=True)
         alpha0 = cross / nsq
         g = mm(table("z_down"), stack_rows(r.reshape(256, 128)))
-        hi, lo = split(g)
-        hilo = jnp.concatenate([hi, lo], axis=1)
-
-        hot = sh[...]
-        y = mm(hilo, jnp.concatenate([hot, hot], axis=0))
-        pick = iota((KZ, NPW_DEV), 0) == lax.bitwise_and(slv[...] + 32, 127)
+        hi, lo = split(jnp.concatenate([g[: 2 * KH], g[2 * KH :]], axis=1))
+        y = mm(jnp.concatenate([hi, lo], axis=0), sh[...])
+        y = y[: 2 * KH] + y[2 * KH :]
+        pick = iota((KH, NPW_DEV), 0) == khi
         for c in range(2):
-            part = jnp.sum(jnp.where(pick, y[c * KZ : (c + 1) * KZ], 0.0), axis=0, keepdims=True)
+            part = jnp.sum(jnp.where(pick, y[c * KH : (c + 1) * KH], 0.0), axis=0, keepdims=True)
             wvec[n, c : c + 1] = part + (kin[...] - alpha0) * coeffs[c, n : n + 1]
         w_re = wvec[n, 0:1]
         w_im = wvec[n, 1:2]
-        sb5[n] = scatter(w_re, w_im)
+        sb5[n] = scatter(w_re, w_im, True)
         send_pw(sb5.at[n], rb5.at[n], A5 + n)
         wsq = w_re * w_re + w_im * w_im
         states.append((nsq, alpha0, total(wsq), total(wsq * kin[...])))
@@ -609,11 +659,13 @@
             V(atom_sites.shape, jnp.int32),
             V((2, 2, NPW_DEV), F32),
             V((4, NG, NG), F32),
-            V((128, NPW_DEV), BF16),
-            V((4 * KZ, NPW_DEV), BF16),
+            V((256, NPW_DEV), BF16),
+            V((NPW_DEV, 256), BF16),
+            V((4 * KH, NPW_DEV), BF16),
             V((1, NPW_DEV), F32),
             V((256, 4096), BF16),
             V((NR, 4096), F32),
+            V((2, 4096), F32),
             V((2, 256, 512), F32),
             V((1, NPW_DEV), jnp.int32),
             V((NP, 128), jnp.int32),
@@ -627,8 +679,8 @@
             V((NB, 16, 512), F32),
             V((16, 512), F32),
             V((8, 8, 128), F32),
-            V((NP, 8, 128), F32),
-            V((NP, 8, 128), F32),
+            V((8 * NP, 128), F32),
+            V((8 * NP, 128), F32),
             V((512, 128), F32),
             V((128, 512), F32),
             V((2, NP, 8, 128), F32),

time: 78.5 us -> 72.7 us (0.926)
  Pallas kernels: 77.7 us -> 71.9 us
    pallas_call x1, Pallas kernels: 76 us -> 70.2 us  [local(): pl.pallas_call(kernel, out_shape=results, in_specs=[hbm] * (5 + len(NAMES...]
where the time goes in v2:
time: 72.7 us; the launch traced here: 72.6 us
  Pallas kernels  71.9 us (99%)
    pallas_call x1, Pallas kernels, local(): pl.pallas_call(kernel, out_shape=results, in_specs=[hbm] * (5 + len(NAMES...  70.2 us
    pallas_call x1, Pallas kernels, local(): pl.pallas_call(copies, out_shape=results, in_specs=[vm, vm], out_specs=(v...  1.71 us

profile of v2, /device:TPU:1, one launch (start us, length us, event | category | flops | bytes accessed | tf_op | source)
XLA Modules:
  0.0 72.6 jit_solution(15197119383123518703)
XLA Ops:
  0.6 70.2 %step.1 = (f32[2,2,3584]{2,1,0:T(2,128)}, f32[4,128,128]{2,1,0:T(8,128)}) custom-call(f32[2,2,3584]{2,1,0:T(2,128)} %coeffs_in.1, f32[2]{0:T(128)} %occ_in.1, s32[24,128]{1,0:T(8,128)} %bitcast.3, s32[28,128]{1,0:T(8,128)} %bitcast.2, s32[3,1000]{1,0:T(4,128)} %atoms_in.1, bf16[256,480]{1,0:T(8,128)(2,1)} %constant.30.clone.refs_0_, ...), custom_call_target="tpu_custom_call" | custom-call | tf_op jit(solution)/shard_map/step/pallas_call | solution.py:649
  70.9 1.7 %results.1 = (f32[2,2,3584]{2,1,0:T(2,128)}, f32[4,128,128]{2,1,0:T(8,128)}) custom-call(f32[2,2,3584]{2,1,0:T(2,128)} %get-tuple-element.4.new_in, f32[4,128,128]{2,1,0:T(8,128)} %get-tuple-element.5.dens_in), custom_call_target="tpu_custom_call" | custom-call | tf_op jit(solution)/shard_map/results/pallas_call | solution.py:705

commit v3 on v2

--- a/solution.py
+++ b/solution.py
@@ -22,6 +22,7 @@
 ST = 96
 KH = 40
 NR = 16
+NQ = NP * ST // 128
 NX = 8 * NR + 16
 TIME_STEP = 0.2
 EPSILON = 1e-06
@@ -34,8 +35,14 @@
 
 A1, RS, A2, A3, AGV, AGD, A4, A5, AR = 0, 2, 3, 4, 5, 6, 7, 9, 11
 N_SEM = 12
-MIX = 13
+PEERS = tuple(sorted(((x, y, c) for x in range(4) for y in range(4) for c in (0, 1) if x or y or c), key=lambda d: (-min(d[0], 4 - d[0]) - min(d[1], 4 - d[1]), (d[0] + 3 * d[1]) % 4, d[2])))
 FAR_FIRST = (4, 3, 5, 2, 6, 1, 7)
+TARGETS = tuple(
+    sorted(
+        ((b, x, h) for x in (2, 1, 3, 0) for h in (1, 0) for b in FAR_FIRST + (0,) if b or x or h),
+        key=lambda d: -min(d[0], 8 - d[0]) - min(d[1], 4 - d[1]) - 2 * d[2],
+    )
+)
 
 
 def parts(x):
@@ -227,6 +234,12 @@
     for k in NAMES:
         loads[k].start()
 
+    at_x, at_y, at_core = lax.div(me, 8), lax.rem(lax.div(me, 2), 4), lax.rem(me, 2)
+
+    def peer(offset):
+        x, y, core = offset
+        return lax.rem(at_x + x, 4) * 8 + lax.rem(at_y + y, 4) * 2 + lax.rem(at_core + core, 2)
+
     due = {}
     gone = {}
 
@@ -234,14 +247,11 @@
         due[k], gone[k] = dst, dst.at[pl.ds(0, NP - 1)]
         pltpu.make_async_copy(src.at[me], dst.at[me], rsem.at[k]).start()
 
-        def one(i, carry):
-            to = lax.rem(me + MIX * i, NP)
+        for offset in PEERS:
+            to = peer(offset)
             pltpu.make_async_remote_copy(
                 src.at[to], dst.at[me], ssem.at[k], rsem.at[k], device_id={"pw": to}, device_id_type=MESH
             ).start()
-            return carry
-
-        lax.fori_loop(1, NP, one, 0)
 
     def send_band(src, dst, whole, k):
         due[k], gone[k] = whole, whole.at[pl.ds(0, whole.shape[0] // NB * (NB - 1))]
@@ -291,25 +301,16 @@
     send_pw(sb1.at[1], rb1.at[1], A1 + 1)
 
     inputs[2].wait()
-    c0, c1, c2 = (cols[pl.ds(i, 8, stride=3), :] for i in range(3))
     lane8 = iota((8, 128), 1)
-    blocks = (
-        c0,
-        jnp.where(lane8 < 32, pltpu.roll(c0, 32, 1), pltpu.roll(c1, 32, 1)),
-        jnp.where(lane8 < 64, pltpu.roll(c1, 64, 1), pltpu.roll(c2, 64, 1)),
-        pltpu.roll(c2, 96, 1),
-    )
-    for i, block in enumerate(blocks):
-        cpad[pl.ds(i, 8, stride=4), :] = jnp.where(lane8 < ST, block, -1)
-    c = cpad[...]
+    c = cols[...]
     xp = lax.bitwise_and(lax.shift_right_arithmetic(c, 7) + 32, 127)
     yp = lax.bitwise_and(c + 32, 127)
-    far_x = jnp.logical_and(c >= 0, xp == 64)
-    far_y = jnp.logical_and(c >= 0, yp == 64)
-    regular = jnp.logical_and(c >= 0, jnp.logical_and(xp < 64, yp < 64))
+    far_x = xp == 64
+    far_y = yp == 64
+    regular = jnp.logical_and(xp < 64, yp < 64)
     r = jnp.where(regular, lax.shift_right_logical(xp, 2), -1)
     q = lax.bitwise_and(xp, 3) * 64 + yp
-    for p in range(NP):
+    for p in range(NQ):
         at = slice(p * 128, (p + 1) * 128)
         mt[:, at] = (iota((NR, 128), 0) == r[p : p + 1]).astype(F32)
         tt[:, at] = (iota((256, 128), 0) == q[p : p + 1]).astype(BF16)
@@ -327,15 +328,22 @@
         g = None
         ends = [jnp.zeros((8, 128), F32), jnp.zeros((8, 128), F32)]
         for p0 in range(0, NP, 4):
+            d0, d1, d2, d3 = (rb[p0 + i] for i in range(4))
+            d1, d2, d3 = pltpu.roll(d1, 96, 1), pltpu.roll(d2, 64, 1), pltpu.roll(d3, 32, 1)
+            packed = (
+                jnp.where(lane8 < 96, d0, d1),
+                jnp.where(lane8 < 64, d1, d2),
+                jnp.where(lane8 < 32, d2, d3),
+            )
             block = []
-            for p in range(p0, p0 + 4):
-                d = rb[p]
+            q0 = p0 // 4 * 3
+            for p, d in enumerate(packed, q0):
                 m = mt[:, p * 128 : (p + 1) * 128]
                 ends = [x + d * ms[i : i + 1, p * 128 : (p + 1) * 128] for i, x in enumerate(ends)]
                 hi = d.astype(BF16).astype(F32)
                 rows = [jnp.broadcast_to(v[i : i + 1], (NR, 128)) * m for v in (hi, d - hi) for i in range(8)]
                 block.append(jnp.concatenate(rows, axis=0).astype(BF16))
-            y = mm_nt(jnp.concatenate(block, axis=1), tt[:, p0 * 128 : (p0 + 4) * 128])
+            y = mm_nt(jnp.concatenate(block, axis=1), tt[:, q0 * 128 : (q0 + 3) * 128])
             g = y if g is None else g + y
         g = g[: 8 * NR] + g[8 * NR :]
         hi = g.astype(BF16).astype(F32)
@@ -394,6 +402,15 @@
     xb[0:8] = xb[0:8] + jnp.where(iota((8, 512), 0) == 0, head, 0.0)
     send_band(lambda to: xb.at[pl.ds(pl.multiple_of(16 * to, 16), 16)], rsb.at[band], rsb, RS)
 
+    c0, c1, c2 = (cols[pl.ds(i, 8, stride=3), :] for i in range(3))
+    blocks = (
+        c0,
+        jnp.where(lane8 < 32, pltpu.roll(c0, 32, 1), pltpu.roll(c1, 32, 1)),
+        jnp.where(lane8 < 64, pltpu.roll(c1, 64, 1), pltpu.roll(c2, 64, 1)),
+        pltpu.roll(c2, 96, 1),
+    )
+    for i, block in enumerate(blocks):
+        cpad[pl.ds(i, 8, stride=4), :] = jnp.where(lane8 < ST, block, -1)
     own = cpad[pl.ds(me, 1), :]
     wx = wrapped(lax.bitwise_and(lax.shift_right_arithmetic(own, 7), 127))
     wy = wrapped(lax.bitwise_and(own, 127))
@@ -449,14 +466,11 @@
     slot_me = pl.ds(pl.multiple_of(8 * me, 8), 8)
     pltpu.make_async_copy(tb.at[mine], rb2.at[slot_me], rsem.at[A2]).start()
 
-    def out_a2(i, carry):
-        to = lax.rem(me + MIX * i, NP)
+    for offset in PEERS:
+        to = peer(offset)
         pltpu.make_async_remote_copy(
             tb.at[lax.div(to, 4)], rb2.at[slot_me], ssem.at[A2], rsem.at[A2], device_id={"pw": to}, device_id_type=MESH
         ).start()
-        return carry
-
-    lax.fori_loop(1, NP, out_a2, 0)
     due[A2], gone[A2] = rb2, rb2.at[pl.ds(0, 8 * (NP - 1))]
 
     arrive(A2)
@@ -476,28 +490,16 @@
     place = pl.ds(pl.multiple_of(8 * turn, 8), 8)
     pltpu.make_async_copy(ub.at[slot_me], rbv.at[place], rsem.at[A3]).start()
 
-    def out_a3(i, offsets):
-        spot = 4 * lax.rem(mine + i, 8) + low
-        for offset in offsets:
-            pltpu.make_async_remote_copy(
-                ub.at[pl.ds(pl.multiple_of(8 * spot, 8), 8)],
-                rbv.at[place],
-                ssem.at[A3],
-                rsem.at[A3],
-                device_id={"band": lax.rem(band + offset, NB), "pw": spot},
-                device_id_type=MESH,
-            ).start()
-
-    def out_far(i, carry):
-        out_a3(i, FAR_FIRST)
-        return carry
-
-    def out_near(i, carry):
-        out_a3(i, (0,))
-        return carry
-
-    lax.fori_loop(0, 8, out_far, 0)
-    lax.fori_loop(1, 8, out_near, 0)
+    for away, x, half in TARGETS:
+        spot = peer((x, 2 * half, 0))
+        pltpu.make_async_remote_copy(
+            ub.at[pl.ds(pl.multiple_of(8 * spot, 8), 8)],
+            rbv.at[place],
+            ssem.at[A3],
+            rsem.at[A3],
+            device_id={"band": lax.rem(band + away, NB), "pw": spot},
+            device_id_type=MESH,
+        ).start()
     due[A3], gone[A3] = rbv, rbv.at[pl.ds(0, 8 * 63)]
     arrive(A3)
     vk = [
@@ -552,8 +554,16 @@
             [jnp.sum(y[k * NR : (k + 1) * NR] * m, axis=0, keepdims=True) for k in range(8)], axis=0
         )
         y = y + ex * ms[0:1] + ey * ms[1:2]
-        for p in range(NP):
-            sb4[n, p] = y[:, p * 128 : (p + 1) * 128] + extra
+        for g in range(NP // 4):
+            t0, t1, t2 = (y[:, (3 * g + i) * 128 : (3 * g + i + 1) * 128] for i in range(3))
+            blocks = (
+                t0,
+                jnp.where(lane8 < 32, pltpu.roll(t0, 32, 1), pltpu.roll(t1, 32, 1)),
+                jnp.where(lane8 < 64, pltpu.roll(t1, 64, 1), pltpu.roll(t2, 64, 1)),
+                pltpu.roll(t2, 96, 1),
+            )
+            for i, block in enumerate(blocks):
+                sb4[n, 4 * g + i] = jnp.where(lane8 < ST, block, extra)
         send_pw(sb4.at[n], rb4.at[n], A4 + n)
 
     at_band = pl.ds(pl.multiple_of(16 * band, 16), 16)
@@ -588,17 +598,14 @@
         f = to_field(rb5.at[n])
         energy = weight * total(pot[...] * (f[:128] * f[:128] + f[128:] * f[128:])) + states[n][3]
         out = out + jnp.where(lane1 == 2 * n, states[n][2], 0.0) + jnp.where(lane1 == 2 * n + 1, energy, 0.0)
-    sbr[...] = out
+    sbr[...] = out[0:1]
     pltpu.make_async_copy(sbr, rbr.at[me], rsem.at[AR]).start()
 
-    def out_ar(i, carry):
-        to = lax.rem(me + i, NP)
+    for offset in PEERS:
+        to = peer(offset)
         pltpu.make_async_remote_copy(
             sbr, rbr.at[me], ssem.at[AR], rsem.at[AR], device_id={"pw": to}, device_id_type=MESH
         ).start()
-        return carry
-
-    lax.fori_loop(1, NP, out_ar, 0)
     due[AR], gone[AR] = rbr, rbr.at[pl.ds(0, NP - 1)]
     arrive(AGD)
     d = plane_inverse(dk[...], "pix") * (1.0 / (NG * NG))
@@ -607,7 +614,7 @@
     dens_copy = pltpu.make_async_copy(dens_val, dens_out, osem.at[0])
     dens_copy.start()
     arrive(AR)
-    ends = jnp.sum(rbr[...], axis=0)[0:1]
+    ends = jnp.sum(rbr[...], axis=0)
     for n in range(2):
         nsq, alpha0 = states[n][0], states[n][1]
         ww = jnp.sum(jnp.where(iota((1, 128), 1) == 2 * n, ends, 0.0), axis=1, keepdims=True)
@@ -663,9 +670,9 @@
             V((NPW_DEV, 256), BF16),
             V((4 * KH, NPW_DEV), BF16),
             V((1, NPW_DEV), F32),
-            V((256, 4096), BF16),
-            V((NR, 4096), F32),
-            V((2, 4096), F32),
+            V((256, NQ * 128), BF16),
+            V((NR, NQ * 128), F32),
+            V((2, NQ * 128), F32),
             V((2, 256, 512), F32),
             V((1, NPW_DEV), jnp.int32),
             V((NP, 128), jnp.int32),
@@ -687,8 +694,8 @@
             V((2, NP, 8, 128), F32),
             V((2, NP, 8, 128), F32),
             V((2, NP, 8, 128), F32),
-            V((8, 128), F32),
-            V((NP, 8, 128), F32),
+            V((1, 128), F32),
+            V((NP, 1, 128), F32),
             V((128, 1024), F32),
             pltpu.SemaphoreType.DMA((N_SEM,)),
             pltpu.SemaphoreType.DMA((N_SEM,)),

time: 72.7 us -> 69.2 us (0.952)
  Pallas kernels: 71.9 us -> 68.4 us
    pallas_call x1, Pallas kernels: 70.2 us -> 66.7 us  [local(): pl.pallas_call(kernel, out_shape=results, in_specs=[hbm] * (5 + len(NAMES...]
where the time goes in v3:
time: 69.2 us; the launch traced here: 69 us
  Pallas kernels  68.4 us (99%)
    pallas_call x1, Pallas kernels, local(): pl.pallas_call(kernel, out_shape=results, in_specs=[hbm] * (5 + len(NAMES...  66.7 us
    pallas_call x1, Pallas kernels, local(): pl.pallas_call(copies, out_shape=results, in_specs=[vm, vm], out_specs=(v...  1.71 us

profile of v3, /device:TPU:1, one launch (start us, length us, event | category | flops | bytes accessed | tf_op | source)
XLA Modules:
  0.0 69.0 jit_solution(15711203776885278005)
XLA Ops:
  0.6 66.7 %step.1 = (f32[2,2,3584]{2,1,0:T(2,128)}, f32[4,128,128]{2,1,0:T(8,128)}) custom-call(f32[2,2,3584]{2,1,0:T(2,128)} %coeffs_in.1, f32[2]{0:T(128)} %occ_in.1, s32[24,128]{1,0:T(8,128)} %bitcast.3, s32[28,128]{1,0:T(8,128)} %bitcast.2, s32[3,1000]{1,0:T(4,128)} %atoms_in.1, bf16[256,480]{1,0:T(8,128)(2,1)} %constant.30.clone.refs_0_, ...), custom_call_target="tpu_custom_call" | custom-call | tf_op jit(solution)/shard_map/step/pallas_call | solution.py:656
  67.3 1.7 %results.1 = (f32[2,2,3584]{2,1,0:T(2,128)}, f32[4,128,128]{2,1,0:T(8,128)}) custom-call(f32[2,2,3584]{2,1,0:T(2,128)} %get-tuple-element.4.new_in, f32[4,128,128]{2,1,0:T(8,128)} %get-tuple-element.5.dens_in), custom_call_target="tpu_custom_call" | custom-call | tf_op jit(solution)/shard_map/results/pallas_call | solution.py:712

commit v4 on v3

--- a/solution.py
+++ b/solution.py
@@ -221,24 +221,18 @@
 
     barrier = pltpu.get_barrier_semaphore()
 
-    def greet_pw(i, carry):
-        pl.semaphore_signal(barrier, inc=1, device_id={"pw": lax.rem(me + i, NP)}, device_id_type=MESH)
-        return carry
-
-    def greet_band(i, carry):
-        pl.semaphore_signal(barrier, inc=1, device_id={"band": lax.rem(band + i, NB)}, device_id_type=MESH)
-        return carry
-
-    lax.fori_loop(1, NP, greet_pw, 0)
-    lax.fori_loop(1, NB, greet_band, 0)
-    for k in NAMES:
-        loads[k].start()
-
     at_x, at_y, at_core = lax.div(me, 8), lax.rem(lax.div(me, 2), 4), lax.rem(me, 2)
 
     def peer(offset):
         x, y, core = offset
         return lax.rem(at_x + x, 4) * 8 + lax.rem(at_y + y, 4) * 2 + lax.rem(at_core + core, 2)
+
+    for offset in PEERS:
+        pl.semaphore_signal(barrier, inc=1, device_id={"pw": peer(offset)}, device_id_type=MESH)
+    for i in FAR_FIRST:
+        pl.semaphore_signal(barrier, inc=1, device_id={"band": lax.rem(band + i, NB)}, device_id_type=MESH)
+    for k in NAMES:
+        loads[k].start()
 
     due = {}
     gone = {}

time: 69.2 us -> 69 us (level)
  no operation moved by 1% of the time
where the time goes in v4:
time: 69 us; the launch traced here: 68.8 us
  Pallas kernels  68.2 us (99%)
    pallas_call x1, Pallas kernels, local(): pl.pallas_call(kernel, out_shape=results, in_specs=[hbm] * (5 + len(NAMES...  66.4 us
    pallas_call x1, Pallas kernels, local(): pl.pallas_call(copies, out_shape=results, in_specs=[vm, vm], out_specs=(v...  1.71 us

profile of v4, /device:TPU:1, one launch (start us, length us, event | category | flops | bytes accessed | tf_op | source)
XLA Modules:
  0.0 68.8 jit_solution(17390230813960336733)
XLA Ops:
  0.6 66.4 %step.1 = (f32[2,2,3584]{2,1,0:T(2,128)}, f32[4,128,128]{2,1,0:T(8,128)}) custom-call(f32[2,2,3584]{2,1,0:T(2,128)} %coeffs_in.1, f32[2]{0:T(128)} %occ_in.1, s32[24,128]{1,0:T(8,128)} %bitcast.3, s32[28,128]{1,0:T(8,128)} %bitcast.2, s32[3,1000]{1,0:T(4,128)} %atoms_in.1, bf16[256,480]{1,0:T(8,128)(2,1)} %constant.30.clone.refs_0_, ...), custom_call_target="tpu_custom_call" | custom-call | tf_op jit(solution)/shard_map/step/pallas_call | solution.py:650
  67.1 1.7 %results.1 = (f32[2,2,3584]{2,1,0:T(2,128)}, f32[4,128,128]{2,1,0:T(8,128)}) custom-call(f32[2,2,3584]{2,1,0:T(2,128)} %get-tuple-element.4.new_in, f32[4,128,128]{2,1,0:T(8,128)} %get-tuple-element.5.dens_in), custom_call_target="tpu_custom_call" | custom-call | tf_op jit(solution)/shard_map/results/pallas_call | solution.py:706
